TPU v7x, 256 devices: a whole 4x4x8 slice. The times are simulated.
256 devices in a mesh: dp: 16 (over y, x), fsdp: 16 (over z, core).
Axes of the slice: x: 4, y: 4, z: 8, core: 2. Of those that a mesh axis runs over, the one named last changes fastest.
Arguments:
- grads: bfloat16 [16, 16, 1408, 2048], P('dp', None, 'fsdp')
- momentum: float32 [16, 1408, 2048], P(None, 'fsdp', 'dp')
- weights: bfloat16 [16, 1408, 2048], P(None, 'fsdp', 'dp'), may hold values from -0.125 to 0.125
Outputs:
- moment_new: float32 [16, 1408, 2048], P(None, 'fsdp', 'dp')
- new_weights: bfloat16 [16, 1408, 2048], P(None, 'fsdp', 'dp')
- update: bfloat16 [16, 1408, 2048], P(None, 'fsdp', 'dp')
All inputs are finite; a program needn't handle non-finite values.
Results may differ from a plain program's by a relative error of at most 0.03.
Values may be sent and summed in bfloat16 or wider, within the bound.
No kernel may reach another device: no remote copies, remote signals or barrier semaphores. Data moves between devices by JAX's collectives and lax.ppermute only.
A program may use at most 64 MiB of HBM per device.

v0:
```python
import functools
import math

import jax
import jax.numpy as jnp
from jax import lax
from jax.experimental import pallas as pl
from jax.experimental.pallas import tpu as pltpu
from jax.sharding import PartitionSpec as P

SIDE = 4
RING = 8
PIECES = RING + 1
LANE = 128
HALVES = 2

MOMENTUM_DECAY = 0.95
LEARN_RATE = 0.02
DECAY_RATE = 0.1
COEF_A = 3.4445
COEF_B = -4.775
COEF_C = 2.0315
EPS_NORM = 1e-07
F32 = jnp.float32
BF16 = jnp.bfloat16
ROWS_BY_ROWS = (((1,), (1,)), ((), ()))
ANYWHERE = pl.BlockSpec(memory_space=pl.ANY)
IN_HBM = pl.BlockSpec(memory_space=pltpu.HBM)
IN_VMEM = pl.BlockSpec(memory_space=pltpu.VMEM)


def move(value, target):
    pairs = []
    for y in range(SIDE):
        for x in range(SIDE):
            for z in range(RING):
                for core in range(2):
                    ty, tx, tz, tc = target(y, x, z, core)
                    there = (((ty % SIDE) * SIDE + tx % SIDE) * RING + tz % RING) * 2 + tc % 2
                    pairs.append((((y * SIDE + x) * RING + z) * 2 + core, there))
    return lax.ppermute(value, ("dp", "fsdp"), pairs)


def first_hop(value, k):
    return move(value, lambda y, x, z, c: (y, x + k, z, c) if c == 0 else (y + k, x, z, c))


def second_hop(value, k):
    return move(value, lambda y, x, z, c: (y + k, x, z, c) if c == 0 else (y, x + k, z, c))


def along_z(value, k):
    return move(value, lambda y, x, z, c: (y, x, z + k, c) if c == 0 else (y, x, z - k, c))


def swap(value):
    return move(value, lambda y, x, z, c: (y, x, z, c + 1))


def cost(flops, size):
    return pl.CostEstimate(flops=flops, bytes_accessed=size, transcendentals=0)


def matrix(k, m):
    place = lax.axis_index("dp")
    y, x = place // SIDE, place % SIDE
    by_x = ((y + m) % SIDE) * SIDE + (x + k) % SIDE
    by_y = ((y + k) % SIDE) * SIDE + (x + m) % SIDE
    return jnp.where(lax.axis_index("fsdp") % 2 == 0, by_x, by_y)


def pack_kernel(wide, wanted, grads, mom, *refs):
    outs, terms, sems = refs[:-2], refs[-2], refs[-1]
    place = lax.axis_index("dp")
    per = wide // LANE
    cols = pl.ds(pl.multiple_of((place % per) * LANE, LANE), LANE)
    copies = []
    for i, (k, half) in enumerate(wanted):
        for m in range(SIDE):
            block = grads.at[0, matrix(k, m), :, pl.ds(half * wide, wide)]
            copies.append(pltpu.make_async_copy(block, outs[i].at[m], sems.at[0, i, m]))
            copies.append(pltpu.make_async_copy(mom.at[matrix(k, m)], terms.at[i, m], sems.at[1, i, m]))
    for copy in copies:
        copy.start()
    for copy in copies:
        copy.wait()
    for i, (_, half) in enumerate(wanted):

        @pl.when(place // per == half)
        def _():
            for m in range(SIDE):
                moment = MOMENTUM_DECAY * terms[i, m] + outs[i][m, :, cols].astype(F32)
                outs[i][m, :, cols] = moment.astype(BF16)


def pack(grads, momentum, wide, wanted, limit):
    rows = grads.shape[2]
    return pl.pallas_call(
        functools.partial(pack_kernel, wide, wanted),
        out_shape=(jax.ShapeDtypeStruct((SIDE, rows, wide), BF16),) * len(wanted),
        in_specs=[IN_HBM, IN_HBM],
        out_specs=(IN_VMEM,) * len(wanted),
        scratch_shapes=[
            pltpu.VMEM((len(wanted), SIDE, rows, LANE), F32),
            pltpu.SemaphoreType.DMA((2, len(wanted), SIDE)),
        ],
        compiler_params=pltpu.CompilerParams(vmem_limit_bytes=limit << 20),
        cost_estimate=cost(0, 4 * SIDE * rows * wide * len(wanted)),
    )(grads, momentum)


def add_kernel(count, split, *refs):
    inputs, outs = refs[: len(refs) - count[1]], refs[len(refs) - count[1] :]
    each = count[0]
    for place in range(len(inputs) // each):
        terms = inputs[place * each : (place + 1) * each]
        for m in range(SIDE):
            total = terms[0][m].astype(F32)
            for term in terms[1:]:
                total = total + term[m].astype(F32)
            if split:
                outs[place * SIDE + m][...] = total.astype(BF16)
            else:
                outs[place][m] = total.astype(BF16)


def add_up(groups, split):
    _, rows, wide = groups[0][0].shape
    if split:
        shape = (jax.ShapeDtypeStruct((rows, wide), BF16),) * (SIDE * len(groups))
    else:
        shape = (jax.ShapeDtypeStruct((SIDE, rows, wide), BF16),) * len(groups)
    inputs = [array for group in groups for array in group]
    return pl.pallas_call(
        functools.partial(add_kernel, (len(groups[0]), len(shape)), split),
        out_shape=shape,
        in_specs=[IN_VMEM] * len(inputs),
        out_specs=(IN_VMEM,) * len(shape),
        compiler_params=pltpu.CompilerParams(vmem_limit_bytes=16 << 20),
        cost_estimate=cost(0, 2 * SIDE * rows * wide * (len(inputs) + len(groups))),
    )(*inputs)


def combine_kernel(part0, part1, part2, part3, blocks, sent):
    for block in range(blocks.shape[0]):
        cols = slice(block * LANE, (block + 1) * LANE)
        total = part0[:, cols].astype(F32) + part1[:, cols].astype(F32)
        total = total + (part2[:, cols].astype(F32) + part3[:, cols].astype(F32))
        rounded = total.astype(BF16)
        blocks[block] = rounded
        sent[:, cols] = rounded


def combine(parts):
    rows, wide = parts[0].shape
    return pl.pallas_call(
        combine_kernel,
        out_shape=(
            jax.ShapeDtypeStruct((wide // LANE, rows, LANE), BF16),
            jax.ShapeDtypeStruct((rows, wide), BF16),
        ),
        in_specs=[IN_VMEM] * SIDE,
        out_specs=(IN_VMEM,) * 2,
        compiler_params=pltpu.CompilerParams(vmem_limit_bytes=16 << 20),
        cost_estimate=cost(0, 12 * rows * wide),
    )(*parts)


def gather(sent, core, whole):
    wide = sent.shape[1]
    same = along_z(sent, 1)
    cross = move(sent, lambda y, x, z, c: (y, x, z - 1, 1) if c == 0 else (y, x, z + 1, 0))
    other = swap(sent)
    chip, one = (
        jnp.concatenate([jnp.where(core == 0, mine, theirs), jnp.where(core == 0, theirs, mine)], axis=0)
        for mine, theirs in ((sent, other), (same, cross))
    )
    two = along_z(one, 1)
    three = along_z(two, 1)
    last = three
    if not whole:
        last = lax.dynamic_slice_in_dim(three, core * (wide // 2), wide // 2, axis=1)
    return [chip, one, swap(one), two, swap(two), three, swap(three), along_z(last, 1)]


def fetch(groups, begin, target, sems):
    core = lax.axis_index("fsdp") % 2
    copies = []
    for index, group in enumerate(groups):
        high, wide = group[0].shape[0], target.shape[1] // HALVES
        for place, piece in enumerate(group, begin):
            row, width, start = min(place, RING - 1) * high, piece.shape[1], index * wide
            if width < wide:
                right = core if place == RING - 1 else 1 - core
                start = pl.multiple_of(start + right * width, LANE)
            into = target.at[pl.ds(row, high), pl.ds(start, width)]
            copies.append(pltpu.make_async_copy(piece, into, sems.at[index, place]))
    for copy in copies:
        copy.start()
    return copies


def wait(copies):
    for copy in copies:
        copy.wait()


def gram_strip(rows, gram, at, end):
    term = lax.dot_general(
        rows[at:end, :], rows[0:end, :], ROWS_BY_ROWS, preferred_element_type=F32
    ).astype(BF16)
    gram[at:end, 0:end] = term
    if at:
        gram[0:at, at:end] = term[:, :at].T


def split(refs, counts):
    first, second = counts
    return (refs[:first], refs[first : first + second]), refs[first + second :]


def gram_kernel(counts, stop, *refs):
    groups, (rows, gram, zero, sems) = split(refs, counts)
    wait(fetch(groups, 0, rows, sems))
    for at in range(0, stop, 256):
        gram_strip(rows, gram, at, min(at + 256, stop))
    zero[...] = jnp.zeros(zero.shape, BF16)


def first_gram(groups, stop):
    high, wide = groups[0][0].shape
    size = RING * high
    pieces = [piece for group in groups for piece in group]
    return pl.pallas_call(
        functools.partial(gram_kernel, [len(group) for group in groups], stop),
        out_shape=(
            jax.ShapeDtypeStruct((size, HALVES * wide), BF16),
            jax.ShapeDtypeStruct((size, size), BF16),
            jax.ShapeDtypeStruct((high, wide // 2), BF16),
        ),
        in_specs=[ANYWHERE] * len(pieces),
        out_specs=(IN_VMEM,) * 3,
        scratch_shapes=[pltpu.SemaphoreType.DMA((HALVES, PIECES))],
        compiler_params=pltpu.CompilerParams(vmem_limit_bytes=24 << 20),
        cost_estimate=cost(stop * stop * wide * HALVES, 2 * len(pieces) * high * wide),
    )(*pieces)


def finish_kernel(counts, start, *refs):
    groups, refs = split(refs, counts)
    moments, (_, _, out, rows, gram, current, result, sems) = refs[:HALVES], refs[HALVES:]
    copies = fetch(groups, RING - 1, rows, sems)
    size, cols = rows.shape
    own = out.shape[2]
    for half, moment in enumerate(moments):
        for block in range(moment.shape[0]):
            out[half * moment.shape[0] + block, 0] = moment[block]
    wait(copies)
    for at in range(start, size, 256):
        gram_strip(rows, gram, at, min(at + 256, size))
    total = jnp.zeros((1, 1), F32)
    for at in range(0, size, LANE):
        term = gram[at : at + LANE, at : at + LANE].astype(F32)
        here = lax.broadcasted_iota(jnp.int32, term.shape, 0)
        there = lax.broadcasted_iota(jnp.int32, term.shape, 1)
        total = total + jnp.sum(jnp.where(here == there, term, 0.0), keepdims=True)
    inverse = 1.0 / (jnp.sqrt(total) + EPS_NORM)

    first = (lax.axis_index("fsdp") % 2) * own
    chip = gram[0 : 2 * own, :].astype(F32)
    gram_rows = jnp.where(first == 0, chip[:own], chip[own:]) * inverse * inverse

    def times_gram(rest):
        rest = (rest * inverse).astype(BF16)
        return jnp.dot(rest, gram[...], preferred_element_type=F32) * inverse

    current[...] = COEF_B * gram_rows + COEF_C * times_gram(gram_rows)
    result[...] = COEF_A * current[...]

    @pl.loop(0, 2)
    def _(step):
        scalar = jnp.where(step == 0, COEF_A, 0.0)
        once = times_gram(current[...]) + scalar * gram_rows
        current[...] = COEF_A * current[...] + COEF_B * once + COEF_C * times_gram(once)
        value = times_gram(current[...]) + COEF_A * scalar * gram_rows
        once = times_gram(value)
        value = COEF_A * value + COEF_B * once + COEF_C * times_gram(once)
        result[...] += jnp.where(step == 0, COEF_B, COEF_C) * value
        current[...] = value

    rest = result[...]
    scalar = COEF_A * COEF_A
    finite = total < jnp.inf
    high = jnp.where(finite, rest * inverse, 0.0).astype(BF16)
    scalar = jnp.where(finite, scalar * inverse, 0.0)
    chip_rows = rows[0 : 2 * own, :].astype(F32)
    own_rows = jnp.where(first == 0, chip_rows[:own], chip_rows[own:])
    for at in range(0, cols, 512):
        term = jnp.dot(high, rows[:, at : at + 512], preferred_element_type=F32)
        term = (term + scalar * own_rows[:, at : at + 512]).astype(BF16)
        for col in range(0, 512, LANE):
            out[(at + col) // LANE, 1] = term[:, col : col + LANE]


def finish(groups, start, moments, before):
    size, cols = before[0].shape
    own = moments[0].shape[1]
    pieces = [piece for group in groups for piece in group]
    inputs = len(pieces) + len(moments)
    return pl.pallas_call(
        functools.partial(finish_kernel, [len(group) for group in groups], start),
        out_shape=(
            jax.ShapeDtypeStruct((cols // LANE, 2, own, LANE), BF16),
            jax.ShapeDtypeStruct((size, cols), BF16),
            jax.ShapeDtypeStruct((size, size), BF16),
        ),
        in_specs=[ANYWHERE] * len(pieces) + [IN_VMEM] * (len(moments) + 2),
        out_specs=(IN_VMEM,) * 3,
        scratch_shapes=[
            pltpu.VMEM((own, size), F32),
            pltpu.VMEM((own, size), F32),
            pltpu.SemaphoreType.DMA((HALVES, PIECES)),
        ],
        input_output_aliases={inputs: 1, inputs + 1: 2},
        compiler_params=pltpu.CompilerParams(vmem_limit_bytes=32 << 20),
        cost_estimate=cost(26 * own * size * size + size * size * cols, 2 * size * (size + cols)),
    )(*pieces, *moments, *before)[0]


def update_kernel(scale, returned, weights, moment_new, new_weights, update):
    moment_new[...] = returned[:, 0].astype(F32)
    direction = scale * returned[:, 1].astype(F32)
    update[...] = direction.astype(BF16)
    kept = weights[...].astype(F32) * (1.0 - LEARN_RATE * DECAY_RATE)
    new_weights[...] = (kept - LEARN_RATE * direction).astype(BF16)


def apply_update(returned, weights, scale):
    shape = weights.shape
    return pl.pallas_call(
        functools.partial(update_kernel, scale),
        out_shape=(
            jax.ShapeDtypeStruct(shape, F32),
            jax.ShapeDtypeStruct(shape, BF16),
            jax.ShapeDtypeStruct(shape, BF16),
        ),
        in_specs=[IN_VMEM] * 2,
        out_specs=(IN_VMEM,) * 3,
        compiler_params=pltpu.CompilerParams(vmem_limit_bytes=16 << 20),
    )(returned, weights)


def body(grads, momentum, weights):
    _, rows_dev, cols_dev = momentum.shape
    rows_total = rows_dev * lax.axis_size("fsdp")
    cols_total = cols_dev * lax.axis_size("dp")
    wide = cols_total // HALVES
    core = lax.axis_index("fsdp") % 2
    up1, down1 = pack(grads, momentum, wide, ((2, 0), (2, 1)), 59)
    up1, down1 = first_hop(up1, 1), first_hop(down1, -1)
    up2, down2 = pack(grads, momentum, wide, ((1, 1), (3, 0)), 59)
    up2, down2 = first_hop(up2, 1), first_hop(down2, -1)
    next_up, next_down, own0, own1 = pack(
        grads, momentum, wide, ((1, 0), (3, 1), (0, 0), (0, 1)), 48
    )
    up3, down3 = add_up(((next_up, up1), (next_down, down1)), False)
    up3, down3 = first_hop(up3, 1), first_hop(down3, -1)

    sums = add_up(((own0, down2, up3), (own1, up2, down3)), True)
    moments, groups = [], []
    for half in range(HALVES):
        parts = sums[SIDE * half : SIDE * (half + 1)]
        moment, sent = combine([parts[0]] + [second_hop(parts[k], k) for k in (1, 2, 3)])
        moments.append(moment)
        groups.append(gather(sent, core, half == 0))
    stop = rows_total * 9 // 11
    *before, zero = first_gram([groups[0][: RING - 1], groups[1][: RING - 1]], stop)
    last = groups[1][RING - 1]
    ends = [groups[0][RING - 1 :], [last, swap(last + zero)]]
    current = finish(ends, stop, moments, before)
    returned = lax.all_to_all(current, "dp", split_axis=0, concat_axis=0, tiled=True)
    return apply_update(returned, weights, 0.2 * math.sqrt(max(rows_total, cols_total)))


def solution(mesh):
    placed = (P("dp", None, "fsdp", None), P(None, "fsdp", "dp"), P(None, "fsdp", "dp"))
    return jax.shard_map(
        body,
        mesh=mesh,
        in_specs=placed,
        out_specs=(P(None, "fsdp", "dp"), P(None, "fsdp", "dp"), P(None, "fsdp", "dp")),
        check_vma=False,
    )
```

profile of v0, /device:TPU:64, one launch (start us, length us, event | category | flops | bytes accessed | tf_op | source)
XLA Modules:
  0.0 117.8 jit_solution(4468990738807008587)
XLA Ops:
  0.6 0.0 copy-start
  0.6 2.9 %shard_map.60 = (bf16[4,88,1024]{2,1,0:T(8,128)(2,1)}, bf16[4,88,1024]{2,1,0:T(8,128)(2,1)}) custom-call(bf16[1,16,88,2048]{3,2,1,0:T(8,128)(2,1)} %grads.5, f32[16,88,128]{2,1,0:T(8,128)} %mom.5), custom_call_target="tpu_custom_call" | custom-call | bytes 2883584 | tf_op jit(solution)/shard_map/pallas_call | solution.py:98
  3.5 1.6 %collective-permute-start.1 = (bf16[4,88,1024]{2,1,0:T(8,128)(2,1)}, bf16[4,88,1024]{2,1,0:T(8,128)(2,1)S(1)}, u32[]{:S(2)}, u32[]{:S(2)}) collective-permute-start(bf16[4,88,1024]{2,1,0:T(8,128)(2,1)} %get-tuple-element.32), channel_id=1, source_target_pairs={{0,16},{1,65},{2,18},{3,67},{4,20},{5,69},{6,22},{7,71},{8,24},{9,... | collective-permute-start | bytes 2162696 | tf_op jit(solution)/shard_map/ppermute | solution.py:41
  5.1 1.7 %collective-permute-start.2 = (bf16[4,88,1024]{2,1,0:T(8,128)(2,1)}, bf16[4,88,1024]{2,1,0:T(8,128)(2,1)S(1)}, u32[]{:S(2)}, u32[]{:S(2)}) collective-permute-start(bf16[4,88,1024]{2,1,0:T(8,128)(2,1)} %get-tuple-element.34), channel_id=1, source_target_pairs={{0,48},{1,193},{2,50},{3,195},{4,52},{5,197},{6,54},{7,199},{8,56}... | collective-permute-start | bytes 2162696 | tf_op jit(solution)/shard_map/ppermute | solution.py:41
  6.9 2.8 %shard_map.59 = (bf16[4,88,1024]{2,1,0:T(8,128)(2,1)}, bf16[4,88,1024]{2,1,0:T(8,128)(2,1)}) custom-call(bf16[1,16,88,2048]{3,2,1,0:T(8,128)(2,1)} %grads.5, f32[16,88,128]{2,1,0:T(8,128)} %mom.5), custom_call_target="tpu_custom_call" | custom-call | bytes 2883584 | tf_op jit(solution)/shard_map/pallas_call | solution.py:98
  9.7 1.6 %collective-permute-start = (bf16[4,88,1024]{2,1,0:T(8,128)(2,1)}, bf16[4,88,1024]{2,1,0:T(8,128)(2,1)S(1)}, u32[]{:S(2)}, u32[]{:S(2)}) collective-permute-start(bf16[4,88,1024]{2,1,0:T(8,128)(2,1)} %get-tuple-element.30), channel_id=1, source_target_pairs={{0,48},{1,193},{2,50},{3,195},{4,52},{5,197},{6,54},{7,199},{8,56}... | collective-permute-start | bytes 2162696 | tf_op jit(solution)/shard_map/ppermute | solution.py:41
  11.3 0.5 collective-permute-start.4
  11.8 2.4 %shard_map.58 = (bf16[4,88,1024]{2,1,0:T(8,128)(2,1)S(1)}, bf16[4,88,1024]{2,1,0:T(8,128)(2,1)S(1)}, bf16[4,88,1024]{2,1,0:T(8,128)(2,1)S(1)}, bf16[4,88,1024]{2,1,0:T(8,128)(2,1)S(1)}) custom-call(bf16[1,16,88,2048]{3,2,1,0:T(8,128)(2,1)} %grads.5, f32[16,88,128]{2,1,0:T(8,128)S(1)} %copy-done), custom_call_target="tpu_custom_call" | custom-call | bytes 5767168 | tf_op jit(solution)/shard_map/pallas_call | solution.py:98
  14.2 2.2 %collective-permute-done.1.refs_1_ = bf16[4,88,1024]{2,1,0:T(8,128)(2,1)S(1)} collective-permute-done((bf16[4,88,1024]{2,1,0:T(8,128)(2,1)}, bf16[4,88,1024]{2,1,0:T(8,128)(2,1)S(1)}, u32[]{:S(2)}, u32[]{:S(2)}) %collective-permute-start.1) | collective-permute-done | bytes 720928 | tf_op jit(solution)/shard_map/ppermute | solution.py:41
  16.3 0.3 collective-permute-done.2.refs_3_
  16.6 0.3 shard_map.61
  16.9 1.6 %collective-permute-start.3 = (bf16[4,88,1024]{2,1,0:T(8,128)(2,1)S(1)}, bf16[4,88,1024]{2,1,0:T(8,128)(2,1)S(1)}, u32[]{:S(2)}, u32[]{:S(2)}) collective-permute-start(bf16[4,88,1024]{2,1,0:T(8,128)(2,1)S(1)} %get-tuple-element.35), channel_id=1, source_target_pairs={{0,16},{1,65},{2,18},{3,67},{4,20},{5,69},{6,22},{7,71},{8,24},{9,... | collective-permute-start | bytes 2162696 | tf_op jit(solution)/shard_map/ppermute | solution.py:41
  18.5 1.7 %collective-permute-start.5 = (bf16[4,88,1024]{2,1,0:T(8,128)(2,1)S(1)}, bf16[4,88,1024]{2,1,0:T(8,128)(2,1)S(1)}, u32[]{:S(2)}, u32[]{:S(2)}) collective-permute-start(bf16[4,88,1024]{2,1,0:T(8,128)(2,1)S(1)} %get-tuple-element.38), channel_id=1, source_target_pairs={{0,48},{1,193},{2,50},{3,195},{4,52},{5,197},{6,54},{7,199},{8,56}... | collective-permute-start | bytes 2162696 | tf_op jit(solution)/shard_map/ppermute | solution.py:41
  20.3 4.1 %collective-permute-done.refs_1_ = bf16[4,88,1024]{2,1,0:T(8,128)(2,1)S(1)} collective-permute-done((bf16[4,88,1024]{2,1,0:T(8,128)(2,1)}, bf16[4,88,1024]{2,1,0:T(8,128)(2,1)S(1)}, u32[]{:S(2)}, u32[]{:S(2)}) %collective-permute-start) | collective-permute-done | bytes 720928 | tf_op jit(solution)/shard_map/ppermute | solution.py:41
  24.3 7.4 %collective-permute-done.3.refs_2_ = bf16[4,88,1024]{2,1,0:T(8,128)(2,1)S(1)} collective-permute-done((bf16[4,88,1024]{2,1,0:T(8,128)(2,1)S(1)}, bf16[4,88,1024]{2,1,0:T(8,128)(2,1)S(1)}, u32[]{:S(2)}, u32[]{:S(2)}) %collective-permute-start.3) | collective-permute-done | bytes 720928 | tf_op jit(solution)/shard_map/ppermute | solution.py:41
  31.8 0.3 collective-permute-done.5.refs_5_
  32.1 0.5 shard_map.62
  32.6 1.7 %collective-permute-start.14 = (bf16[88,1024]{1,0:T(8,128)(2,1)S(1)}, bf16[88,1024]{1,0:T(8,128)(2,1)S(1)}, u32[]{:S(2)}, u32[]{:S(2)}) collective-permute-start(bf16[88,1024]{1,0:T(8,128)(2,1)S(1)} %get-tuple-element.45), channel_id=1, source_target_pairs={{0,64},{1,17},{2,66},{3,19},{4,68},{5,21},{6,70},{7,23},{8,72},{9,... | collective-permute-start | bytes 540680 | tf_op jit(solution)/shard_map/ppermute | solution.py:41
  34.2 2.9 %collective-permute-start.15 = (bf16[88,1024]{1,0:T(8,128)(2,1)S(1)}, bf16[88,1024]{1,0:T(8,128)(2,1)S(1)}, u32[]{:S(2)}, u32[]{:S(2)}) collective-permute-start(bf16[88,1024]{1,0:T(8,128)(2,1)S(1)} %get-tuple-element.46), channel_id=1, source_target_pairs={{0,128},{1,33},{2,130},{3,35},{4,132},{5,37},{6,134},{7,39},{8,136... | collective-permute-start | bytes 540680 | tf_op jit(solution)/shard_map/ppermute | solution.py:41
  37.1 1.3 %collective-permute-start.16 = (bf16[88,1024]{1,0:T(8,128)(2,1)S(1)}, bf16[88,1024]{1,0:T(8,128)(2,1)S(1)}, u32[]{:S(2)}, u32[]{:S(2)}) collective-permute-start(bf16[88,1024]{1,0:T(8,128)(2,1)S(1)} %get-tuple-element.47), channel_id=1, source_target_pairs={{0,192},{1,49},{2,194},{3,51},{4,196},{5,53},{6,198},{7,55},{8,200... | collective-permute-start | bytes 540680 | tf_op jit(solution)/shard_map/ppermute | solution.py:41
  38.5 0.7 collective-permute-start.6
  39.2 0.8 collective-permute-start.7
  39.9 0.0 collective-permute-done.14.part1
  39.9 1.9 %collective-permute-start.8 = (bf16[88,1024]{1,0:T(8,128)(2,1)S(1)}, bf16[88,1024]{1,0:T(8,128)(2,1)S(1)}, u32[]{:S(2)}, u32[]{:S(2)}) collective-permute-start(bf16[88,1024]{1,0:T(8,128)(2,1)S(1)} %get-tuple-element.42), channel_id=1, source_target_pairs={{0,192},{1,49},{2,194},{3,51},{4,196},{5,53},{6,198},{7,55},{8,200... | collective-permute-start | bytes 540680 | tf_op jit(solution)/shard_map/ppermute | solution.py:41
  41.8 0.7 collective-permute-done.15.part2
  42.5 0.1 collective-permute-done.16.part3
  42.6 0.1 shard_map.64
  42.8 0.1 collective-permute-start.18
  42.9 2.0 %collective-permute-start.17 = (bf16[88,1024]{1,0:T(8,128)(2,1)S(1)}, bf16[88,1024]{1,0:T(8,128)(2,1)S(1)}, u32[]{:S(2)}, u32[]{:S(2)}) collective-permute-start(bf16[88,1024]{1,0:T(8,128)(2,1)S(1)} %get-tuple-element.48), channel_id=1, source_target_pairs={{0,2},{1,15},{2,4},{3,1},{4,6},{5,3},{6,8},{7,5},{8,10},{9,7},{10,... | collective-permute-start | bytes 540680 | tf_op jit(solution)/shard_map/ppermute | solution.py:41
  44.9 2.3 %collective-permute-done.6.part1 = bf16[88,1024]{1,0:T(8,128)(2,1)S(1)} collective-permute-done((bf16[88,1024]{1,0:T(8,128)(2,1)S(1)}, bf16[88,1024]{1,0:T(8,128)(2,1)S(1)}, u32[]{:S(2)}, u32[]{:S(2)}) %collective-permute-start.6) | collective-permute-done | bytes 180256 | tf_op jit(solution)/shard_map/ppermute | solution.py:41
  47.1 0.0 collective-permute-done.7.part2
  47.1 0.9 collective-permute-done.8.part3
  48.0 0.1 shard_map.63
  48.2 0.3 collective-permute-start.10
  48.4 2.0 %collective-permute-start.9 = (bf16[88,1024]{1,0:T(8,128)(2,1)S(1)}, bf16[88,1024]{1,0:T(8,128)(2,1)S(1)}, u32[]{:S(2)}, u32[]{:S(2)}) collective-permute-start(bf16[88,1024]{1,0:T(8,128)(2,1)S(1)} %get-tuple-element.43), channel_id=1, source_target_pairs={{0,2},{1,15},{2,4},{3,1},{4,6},{5,3},{6,8},{7,5},{8,10},{9,7},{10,... | collective-permute-start | bytes 540680 | tf_op jit(solution)/shard_map/ppermute | solution.py:41
  50.5 3.2 %collective-permute-start.19 = (bf16[176,1024]{1,0:T(8,128)(2,1)S(1)}, bf16[176,1024]{1,0:T(8,128)(2,1)S(1)}, u32[]{:S(2)}, u32[]{:S(2)}) collective-permute-start(bf16[176,1024]{1,0:T(8,128)(2,1)S(1)} %pad_maximum_fusion.1.refs_8_), channel_id=1, source_target_pairs={{0,2},{1,15},{2,4},{3,1},{4,6},{5,3},{6,8},{7,5},{8,10},{9,7},{10,... | collective-permute-start | bytes 1081352 | tf_op jit(solution)/shard_map/ppermute | solution.py:41
  53.7 0.9 collective-permute-done.10
  54.7 0.6 collective-permute-done.9
  55.3 2.6 %collective-permute-start.11 = (bf16[176,1024]{1,0:T(8,128)(2,1)S(1)}, bf16[176,1024]{1,0:T(8,128)(2,1)S(1)}, u32[]{:S(2)}, u32[]{:S(2)}) collective-permute-start(bf16[176,1024]{1,0:T(8,128)(2,1)S(1)} %pad_maximum_fusion.refs_1_), channel_id=1, source_target_pairs={{0,2},{1,15},{2,4},{3,1},{4,6},{5,3},{6,8},{7,5},{8,10},{9,7},{10,... | collective-permute-start | bytes 1081352 | tf_op jit(solution)/shard_map/ppermute | solution.py:41
  58.0 0.5 collective-permute-start.27
  58.5 0.6 collective-permute-done.19.refs_10_
  59.1 3.1 %collective-permute-start.20 = (bf16[176,1024]{1,0:T(8,128)(2,1)S(1)}, bf16[176,1024]{1,0:T(8,128)(2,1)S(1)}, u32[]{:S(2)}, u32[]{:S(2)}) collective-permute-start(bf16[176,1024]{1,0:T(8,128)(2,1)S(1)} %collective-permute-done.19.refs_10_), channel_id=1, source_target_pairs={{0,2},{1,15},{2,4},{3,1},{4,6},{5,3},{6,8},{7,5},{8,10},{9,7},{10,... | collective-permute-start | bytes 1081352 | tf_op jit(solution)/shard_map/ppermute | solution.py:41
  62.2 0.8 collective-permute-done.11.refs_3_
  63.0 3.6 %collective-permute-start.12 = (bf16[176,1024]{1,0:T(8,128)(2,1)S(1)}, bf16[176,1024]{1,0:T(8,128)(2,1)S(1)}, u32[]{:S(2)}, u32[]{:S(2)}) collective-permute-start(bf16[176,1024]{1,0:T(8,128)(2,1)S(1)} %collective-permute-done.11.refs_3_), channel_id=1, source_target_pairs={{0,2},{1,15},{2,4},{3,1},{4,6},{5,3},{6,8},{7,5},{8,10},{9,7},{10,... | collective-permute-start | bytes 1081352 | tf_op jit(solution)/shard_map/ppermute | solution.py:41
  66.6 0.5 collective-permute-start.23
  67.2 0.9 collective-permute-done.26
  68.0 0.1 collective-permute-start.28
  68.2 0.0 collective-permute-done.27.refs_9_
  68.2 0.4 collective-permute-start.24
  68.6 0.0 collective-permute-done.20.refs_12_
  68.6 0.1 collective-permute-start.29
  68.7 2.9 %collective-permute-done.12.refs_5_ = bf16[176,1024]{1,0:T(8,128)(2,1)S(1)} collective-permute-done((bf16[176,1024]{1,0:T(8,128)(2,1)S(1)}, bf16[176,1024]{1,0:T(8,128)(2,1)S(1)}, u32[]{:S(2)}, u32[]{:S(2)}) %collective-permute-start.12) | collective-permute-done | bytes 360480 | tf_op jit(solution)/shard_map/ppermute | solution.py:41
  71.6 0.1 collective-permute-start.25
  71.8 0.0 collective-permute-done.23.refs_2_
  71.8 3.7 %collective-permute-start.21 = (bf16[176,512]{1,0:T(8,128)(2,1)S(1)}, bf16[176,512]{1,0:T(8,128)(2,1)S(1)}, u32[]{:S(2)}, u32[]{:S(2)}) collective-permute-start(bf16[176,512]{1,0:T(8,128)(2,1)S(1)} %constant_dynamic-slice_fusion), channel_id=1, source_target_pairs={{0,2},{1,15},{2,4},{3,1},{4,6},{5,3},{6,8},{7,5},{8,10},{9,7},{10,... | collective-permute-start | bytes 540680 | tf_op jit(solution)/shard_map/ppermute | solution.py:41
  75.5 0.0 collective-permute-done.28.refs_11_
  75.5 3.7 %collective-permute-start.13 = (bf16[176,1024]{1,0:T(8,128)(2,1)S(1)}, bf16[176,1024]{1,0:T(8,128)(2,1)S(1)}, u32[]{:S(2)}, u32[]{:S(2)}) collective-permute-start(bf16[176,1024]{1,0:T(8,128)(2,1)S(1)} %collective-permute-done.12.refs_5_), channel_id=1, source_target_pairs={{0,2},{1,15},{2,4},{3,1},{4,6},{5,3},{6,8},{7,5},{8,10},{9,7},{10,... | collective-permute-start | bytes 1081352 | tf_op jit(solution)/shard_map/ppermute | solution.py:41
  79.2 0.0 collective-permute-done.24.refs_4_
  79.2 5.0 %shard_map.65 = (bf16[1408,2048]{1,0:T(8,128)(2,1)S(1)}, bf16[1408,1408]{1,0:T(8,128)(2,1)S(1)}, bf16[176,512]{1,0:T(8,128)(2,1)S(1)}) custom-call(bf16[176,1024]{1,0:T(8,128)(2,1)S(1)} %get-tuple-element.63.refs_0_, bf16[176,1024]{1,0:T(8,128)(2,1)S(1)} %pad_maximum_fusion.refs_1_, bf16[176,1024]{1,0:T(8,128)(2,1)S(1)} %collective-permute-done.23.refs_2_, ...), custom_call_target="tpu_custom_call" | custom-call | flops 2717908992 | bytes 5046272 | tf_op jit(solution)/shard_map/pallas_call | solution.py:234
  84.3 0.1 collective-permute-start.30
  84.4 1.4 %collective-permute-done.30.refs_2_ = bf16[176,512]{1,0:T(8,128)(2,1)S(1)} collective-permute-done((bf16[176,512]{1,0:T(8,128)(2,1)S(1)}, bf16[176,512]{1,0:T(8,128)(2,1)S(1)}, u32[]{:S(2)}, u32[]{:S(2)}) %collective-permute-start.30) | collective-permute-done | bytes 180256 | tf_op jit(solution)/shard_map/ppermute | solution.py:41
  85.8 10.8 %shard_map.66 = (bf16[16,2,88,128]{3,2,1,0:T(8,128)(2,1)S(1)}, bf16[1408,2048]{1,0:T(8,128)(2,1)S(1)}, bf16[1408,1408]{1,0:T(8,128)(2,1)S(1)}) custom-call(bf16[176,1024]{1,0:T(8,128)(2,1)S(1)} %collective-permute-done.13.refs_0_, bf16[176,512]{1,0:T(8,128)(2,1)S(1)} %collective-permute-done.21.refs_1_, ...), custom_call_target="tpu_custom_call", output_to_operand_aliasing={{1}: (5, {}), {2}: (6, {})} | custom-call | flops 8595963904 | bytes 9732096 | tf_op jit(solution)/shard_map/pallas_call | solution.py:310
  96.6 20.0 %all_to_all.5.returned = bf16[16,2,88,128]{3,2,1,0:T(8,128)(2,1)S(1)} all-to-all(bf16[16,2,88,128]{3,2,1,0:T(8,128)(2,1)S(1)} %get-tuple-element.54), channel_id=1, replica_groups=mesh['dp'=16,'fsdp'=16] {'dp'}, dimensions={0} | all-to-all | bytes 1441792 | tf_op jit(solution)/shard_map/all_to_all | solution.py:381
  116.6 1.2 %shard_map.67 = (f32[16,88,128]{2,1,0:T(8,128)}, bf16[16,88,128]{2,1,0:T(8,128)(2,1)}, bf16[16,88,128]{2,1,0:T(8,128)(2,1)}) custom-call(bf16[16,2,88,128]{3,2,1,0:T(8,128)(2,1)S(1)} %all_to_all.5.returned, bf16[16,88,128]{2,1,0:T(8,128)(2,1)S(1)} %copy-done.1), custom_call_target="tpu_custom_call" | custom-call | tf_op jit(solution)/shard_map/pallas_call | solution.py:340
  (22 shorter events, 0.3 us)
Async XLA Ops:
  0.6 11.2 %copy-start = (f32[16,88,128]{2,1,0:T(8,128)S(1)}, f32[16,88,128]{2,1,0:T(8,128)}, u32[]{:S(2)}) copy-start(f32[16,88,128]{2,1,0:T(8,128)} %mom.5) | copy-start | bytes 2162692
  3.5 12.8 %collective-permute-start.1 = (bf16[4,88,1024]{2,1,0:T(8,128)(2,1)}, bf16[4,88,1024]{2,1,0:T(8,128)(2,1)S(1)}, u32[]{:S(2)}, u32[]{:S(2)}) collective-permute-start(bf16[4,88,1024]{2,1,0:T(8,128)(2,1)} %get-tuple-element.32), channel_id=1, source_target_pairs={{0,16},{1,65},{2,18},{3,67},{4,20},{5,69},{6,22},{7,71},{8,24},{9,... | collective-permute-start | bytes 2162696 | tf_op jit(solution)/shard_map/ppermute | solution.py:41
  5.1 11.5 %collective-permute-start.2 = (bf16[4,88,1024]{2,1,0:T(8,128)(2,1)}, bf16[4,88,1024]{2,1,0:T(8,128)(2,1)S(1)}, u32[]{:S(2)}, u32[]{:S(2)}) collective-permute-start(bf16[4,88,1024]{2,1,0:T(8,128)(2,1)} %get-tuple-element.34), channel_id=1, source_target_pairs={{0,48},{1,193},{2,50},{3,195},{4,52},{5,197},{6,54},{7,199},{8,56}... | collective-permute-start | bytes 2162696 | tf_op jit(solution)/shard_map/ppermute | solution.py:41
  9.7 14.7 %collective-permute-start = (bf16[4,88,1024]{2,1,0:T(8,128)(2,1)}, bf16[4,88,1024]{2,1,0:T(8,128)(2,1)S(1)}, u32[]{:S(2)}, u32[]{:S(2)}) collective-permute-start(bf16[4,88,1024]{2,1,0:T(8,128)(2,1)} %get-tuple-element.30), channel_id=1, source_target_pairs={{0,48},{1,193},{2,50},{3,195},{4,52},{5,197},{6,54},{7,199},{8,56}... | collective-permute-start | bytes 2162696 | tf_op jit(solution)/shard_map/ppermute | solution.py:41
  11.3 13.0 %collective-permute-start.4 = (bf16[4,88,1024]{2,1,0:T(8,128)(2,1)}, bf16[4,88,1024]{2,1,0:T(8,128)(2,1)S(1)}, u32[]{:S(2)}, u32[]{:S(2)}) collective-permute-start(bf16[4,88,1024]{2,1,0:T(8,128)(2,1)} %get-tuple-element.37), channel_id=1, source_target_pairs={{0,16},{1,65},{2,18},{3,67},{4,20},{5,69},{6,22},{7,71},{8,24},{9,... | collective-permute-start | bytes 2162696 | tf_op jit(solution)/shard_map/ppermute | solution.py:41
  16.9 14.8 %collective-permute-start.3 = (bf16[4,88,1024]{2,1,0:T(8,128)(2,1)S(1)}, bf16[4,88,1024]{2,1,0:T(8,128)(2,1)S(1)}, u32[]{:S(2)}, u32[]{:S(2)}) collective-permute-start(bf16[4,88,1024]{2,1,0:T(8,128)(2,1)S(1)} %get-tuple-element.35), channel_id=1, source_target_pairs={{0,16},{1,65},{2,18},{3,67},{4,20},{5,69},{6,22},{7,71},{8,24},{9,... | collective-permute-start | bytes 2162696 | tf_op jit(solution)/shard_map/ppermute | solution.py:41
  18.5 13.5 %collective-permute-start.5 = (bf16[4,88,1024]{2,1,0:T(8,128)(2,1)S(1)}, bf16[4,88,1024]{2,1,0:T(8,128)(2,1)S(1)}, u32[]{:S(2)}, u32[]{:S(2)}) collective-permute-start(bf16[4,88,1024]{2,1,0:T(8,128)(2,1)S(1)} %get-tuple-element.38), channel_id=1, source_target_pairs={{0,48},{1,193},{2,50},{3,195},{4,52},{5,197},{6,54},{7,199},{8,56}... | collective-permute-start | bytes 2162696 | tf_op jit(solution)/shard_map/ppermute | solution.py:41
  32.6 7.4 %collective-permute-start.14 = (bf16[88,1024]{1,0:T(8,128)(2,1)S(1)}, bf16[88,1024]{1,0:T(8,128)(2,1)S(1)}, u32[]{:S(2)}, u32[]{:S(2)}) collective-permute-start(bf16[88,1024]{1,0:T(8,128)(2,1)S(1)} %get-tuple-element.45), channel_id=1, source_target_pairs={{0,64},{1,17},{2,66},{3,19},{4,68},{5,21},{6,70},{7,23},{8,72},{9,... | collective-permute-start | bytes 540680 | tf_op jit(solution)/shard_map/ppermute | solution.py:41
  34.2 8.3 %collective-permute-start.15 = (bf16[88,1024]{1,0:T(8,128)(2,1)S(1)}, bf16[88,1024]{1,0:T(8,128)(2,1)S(1)}, u32[]{:S(2)}, u32[]{:S(2)}) collective-permute-start(bf16[88,1024]{1,0:T(8,128)(2,1)S(1)} %get-tuple-element.46), channel_id=1, source_target_pairs={{0,128},{1,33},{2,130},{3,35},{4,132},{5,37},{6,134},{7,39},{8,136... | collective-permute-start | bytes 540680 | tf_op jit(solution)/shard_map/ppermute | solution.py:41
  37.1 5.5 %collective-permute-start.16 = (bf16[88,1024]{1,0:T(8,128)(2,1)S(1)}, bf16[88,1024]{1,0:T(8,128)(2,1)S(1)}, u32[]{:S(2)}, u32[]{:S(2)}) collective-permute-start(bf16[88,1024]{1,0:T(8,128)(2,1)S(1)} %get-tuple-element.47), channel_id=1, source_target_pairs={{0,192},{1,49},{2,194},{3,51},{4,196},{5,53},{6,198},{7,55},{8,200... | collective-permute-start | bytes 540680 | tf_op jit(solution)/shard_map/ppermute | solution.py:41
  38.5 8.6 %collective-permute-start.6 = (bf16[88,1024]{1,0:T(8,128)(2,1)S(1)}, bf16[88,1024]{1,0:T(8,128)(2,1)S(1)}, u32[]{:S(2)}, u32[]{:S(2)}) collective-permute-start(bf16[88,1024]{1,0:T(8,128)(2,1)S(1)} %get-tuple-element.40), channel_id=1, source_target_pairs={{0,64},{1,17},{2,66},{3,19},{4,68},{5,21},{6,70},{7,23},{8,72},{9,... | collective-permute-start | bytes 540680 | tf_op jit(solution)/shard_map/ppermute | solution.py:41
  39.2 8.0 %collective-permute-start.7 = (bf16[88,1024]{1,0:T(8,128)(2,1)S(1)}, bf16[88,1024]{1,0:T(8,128)(2,1)S(1)}, u32[]{:S(2)}, u32[]{:S(2)}) collective-permute-start(bf16[88,1024]{1,0:T(8,128)(2,1)S(1)} %get-tuple-element.41), channel_id=1, source_target_pairs={{0,128},{1,33},{2,130},{3,35},{4,132},{5,37},{6,134},{7,39},{8,136... | collective-permute-start | bytes 540680 | tf_op jit(solution)/shard_map/ppermute | solution.py:41
  39.9 8.1 %collective-permute-start.8 = (bf16[88,1024]{1,0:T(8,128)(2,1)S(1)}, bf16[88,1024]{1,0:T(8,128)(2,1)S(1)}, u32[]{:S(2)}, u32[]{:S(2)}) collective-permute-start(bf16[88,1024]{1,0:T(8,128)(2,1)S(1)} %get-tuple-element.42), channel_id=1, source_target_pairs={{0,192},{1,49},{2,194},{3,51},{4,196},{5,53},{6,198},{7,55},{8,200... | collective-permute-start | bytes 540680 | tf_op jit(solution)/shard_map/ppermute | solution.py:41
  42.8 7.7 %collective-permute-start.18 = (bf16[88,1024]{1,0:T(8,128)(2,1)S(1)}, bf16[88,1024]{1,0:T(8,128)(2,1)S(1)}, u32[]{:S(2)}, u32[]{:S(2)}) collective-permute-start(bf16[88,1024]{1,0:T(8,128)(2,1)S(1)} %get-tuple-element.48), channel_id=1, source_target_pairs={{0,15},{1,2},{2,1},{3,4},{4,3},{5,6},{6,5},{7,8},{8,7},{9,10},{10,... | collective-permute-start | bytes 540680 | tf_op jit(solution)/shard_map/ppermute | solution.py:41
  42.9 7.6 %collective-permute-start.17 = (bf16[88,1024]{1,0:T(8,128)(2,1)S(1)}, bf16[88,1024]{1,0:T(8,128)(2,1)S(1)}, u32[]{:S(2)}, u32[]{:S(2)}) collective-permute-start(bf16[88,1024]{1,0:T(8,128)(2,1)S(1)} %get-tuple-element.48), channel_id=1, source_target_pairs={{0,2},{1,15},{2,4},{3,1},{4,6},{5,3},{6,8},{7,5},{8,10},{9,7},{10,... | collective-permute-start | bytes 540680 | tf_op jit(solution)/shard_map/ppermute | solution.py:41
  48.2 6.5 %collective-permute-start.10 = (bf16[88,1024]{1,0:T(8,128)(2,1)S(1)}, bf16[88,1024]{1,0:T(8,128)(2,1)S(1)}, u32[]{:S(2)}, u32[]{:S(2)}) collective-permute-start(bf16[88,1024]{1,0:T(8,128)(2,1)S(1)} %get-tuple-element.43), channel_id=1, source_target_pairs={{0,15},{1,2},{2,1},{3,4},{4,3},{5,6},{6,5},{7,8},{8,7},{9,10},{10,... | collective-permute-start | bytes 540680 | tf_op jit(solution)/shard_map/ppermute | solution.py:41
  48.4 6.8 %collective-permute-start.9 = (bf16[88,1024]{1,0:T(8,128)(2,1)S(1)}, bf16[88,1024]{1,0:T(8,128)(2,1)S(1)}, u32[]{:S(2)}, u32[]{:S(2)}) collective-permute-start(bf16[88,1024]{1,0:T(8,128)(2,1)S(1)} %get-tuple-element.43), channel_id=1, source_target_pairs={{0,2},{1,15},{2,4},{3,1},{4,6},{5,3},{6,8},{7,5},{8,10},{9,7},{10,... | collective-permute-start | bytes 540680 | tf_op jit(solution)/shard_map/ppermute | solution.py:41
  50.5 8.6 %collective-permute-start.19 = (bf16[176,1024]{1,0:T(8,128)(2,1)S(1)}, bf16[176,1024]{1,0:T(8,128)(2,1)S(1)}, u32[]{:S(2)}, u32[]{:S(2)}) collective-permute-start(bf16[176,1024]{1,0:T(8,128)(2,1)S(1)} %pad_maximum_fusion.1.refs_8_), channel_id=1, source_target_pairs={{0,2},{1,15},{2,4},{3,1},{4,6},{5,3},{6,8},{7,5},{8,10},{9,7},{10,... | collective-permute-start | bytes 1081352 | tf_op jit(solution)/shard_map/ppermute | solution.py:41
  55.3 7.7 %collective-permute-start.11 = (bf16[176,1024]{1,0:T(8,128)(2,1)S(1)}, bf16[176,1024]{1,0:T(8,128)(2,1)S(1)}, u32[]{:S(2)}, u32[]{:S(2)}) collective-permute-start(bf16[176,1024]{1,0:T(8,128)(2,1)S(1)} %pad_maximum_fusion.refs_1_), channel_id=1, source_target_pairs={{0,2},{1,15},{2,4},{3,1},{4,6},{5,3},{6,8},{7,5},{8,10},{9,7},{10,... | collective-permute-start | bytes 1081352 | tf_op jit(solution)/shard_map/ppermute | solution.py:41
  58.0 8.6 %collective-permute-start.22 = (bf16[88,1024]{1,0:T(8,128)(2,1)S(1)}, bf16[88,1024]{1,0:T(8,128)(2,1)S(1)}, u32[]{:S(2)}, u32[]{:S(2)}) collective-permute-start(bf16[88,1024]{1,0:T(8,128)(2,1)S(1)} %get-tuple-element.43), channel_id=1, source_target_pairs={{0,1},{1,0},{2,3},{3,2},{4,5},{5,4},{6,7},{7,6},{8,9},{9,8},{10,11... | collective-permute-start | bytes 540680 | tf_op jit(solution)/shard_map/ppermute | solution.py:41
  58.0 10.2 %collective-permute-start.27 = (bf16[176,1024]{1,0:T(8,128)(2,1)S(1)}, bf16[176,1024]{1,0:T(8,128)(2,1)S(1)}, u32[]{:S(2)}, u32[]{:S(2)}) collective-permute-start(bf16[176,1024]{1,0:T(8,128)(2,1)S(1)} %pad_maximum_fusion.1.refs_8_), channel_id=1, source_target_pairs={{0,1},{1,0},{2,3},{3,2},{4,5},{5,4},{6,7},{7,6},{8,9},{9,8},{10,11... | collective-permute-start | bytes 1081352 | tf_op jit(solution)/shard_map/ppermute | solution.py:41
  59.1 9.4 %collective-permute-start.20 = (bf16[176,1024]{1,0:T(8,128)(2,1)S(1)}, bf16[176,1024]{1,0:T(8,128)(2,1)S(1)}, u32[]{:S(2)}, u32[]{:S(2)}) collective-permute-start(bf16[176,1024]{1,0:T(8,128)(2,1)S(1)} %collective-permute-done.19.refs_10_), channel_id=1, source_target_pairs={{0,2},{1,15},{2,4},{3,1},{4,6},{5,3},{6,8},{7,5},{8,10},{9,7},{10,... | collective-permute-start | bytes 1081352 | tf_op jit(solution)/shard_map/ppermute | solution.py:41
  63.0 8.6 %collective-permute-start.12 = (bf16[176,1024]{1,0:T(8,128)(2,1)S(1)}, bf16[176,1024]{1,0:T(8,128)(2,1)S(1)}, u32[]{:S(2)}, u32[]{:S(2)}) collective-permute-start(bf16[176,1024]{1,0:T(8,128)(2,1)S(1)} %collective-permute-done.11.refs_3_), channel_id=1, source_target_pairs={{0,2},{1,15},{2,4},{3,1},{4,6},{5,3},{6,8},{7,5},{8,10},{9,7},{10,... | collective-permute-start | bytes 1081352 | tf_op jit(solution)/shard_map/ppermute | solution.py:41
  66.6 1.4 %collective-permute-start.26 = (bf16[88,1024]{1,0:T(8,128)(2,1)S(1)}, bf16[88,1024]{1,0:T(8,128)(2,1)S(1)}, u32[]{:S(2)}, u32[]{:S(2)}) collective-permute-start(bf16[88,1024]{1,0:T(8,128)(2,1)S(1)} %get-tuple-element.48), channel_id=1, source_target_pairs={{0,1},{1,0},{2,3},{3,2},{4,5},{5,4},{6,7},{7,6},{8,9},{9,8},{10,11... | collective-permute-start | bytes 540680 | tf_op jit(solution)/shard_map/ppermute | solution.py:41
  66.6 5.1 %collective-permute-start.23 = (bf16[176,1024]{1,0:T(8,128)(2,1)S(1)}, bf16[176,1024]{1,0:T(8,128)(2,1)S(1)}, u32[]{:S(2)}, u32[]{:S(2)}) collective-permute-start(bf16[176,1024]{1,0:T(8,128)(2,1)S(1)} %pad_maximum_fusion.refs_1_), channel_id=1, source_target_pairs={{0,1},{1,0},{2,3},{3,2},{4,5},{5,4},{6,7},{7,6},{8,9},{9,8},{10,11... | collective-permute-start | bytes 1081352 | tf_op jit(solution)/shard_map/ppermute | solution.py:41
  68.0 7.4 %collective-permute-start.28 = (bf16[176,1024]{1,0:T(8,128)(2,1)S(1)}, bf16[176,1024]{1,0:T(8,128)(2,1)S(1)}, u32[]{:S(2)}, u32[]{:S(2)}) collective-permute-start(bf16[176,1024]{1,0:T(8,128)(2,1)S(1)} %collective-permute-done.19.refs_10_), channel_id=1, source_target_pairs={{0,1},{1,0},{2,3},{3,2},{4,5},{5,4},{6,7},{7,6},{8,9},{9,8},{10,11... | collective-permute-start | bytes 1081352 | tf_op jit(solution)/shard_map/ppermute | solution.py:41
  68.2 11.0 %collective-permute-start.24 = (bf16[176,1024]{1,0:T(8,128)(2,1)S(1)}, bf16[176,1024]{1,0:T(8,128)(2,1)S(1)}, u32[]{:S(2)}, u32[]{:S(2)}) collective-permute-start(bf16[176,1024]{1,0:T(8,128)(2,1)S(1)} %collective-permute-done.11.refs_3_), channel_id=1, source_target_pairs={{0,1},{1,0},{2,3},{3,2},{4,5},{5,4},{6,7},{7,6},{8,9},{9,8},{10,11... | collective-permute-start | bytes 1081352 | tf_op jit(solution)/shard_map/ppermute | solution.py:41
  68.6 10.6 %collective-permute-start.29 = (bf16[176,1024]{1,0:T(8,128)(2,1)S(1)}, bf16[176,1024]{1,0:T(8,128)(2,1)S(1)}, u32[]{:S(2)}, u32[]{:S(2)}) collective-permute-start(bf16[176,1024]{1,0:T(8,128)(2,1)S(1)} %collective-permute-done.20.refs_12_), channel_id=1, source_target_pairs={{0,1},{1,0},{2,3},{3,2},{4,5},{5,4},{6,7},{7,6},{8,9},{9,8},{10,11... | collective-permute-start | bytes 1081352 | tf_op jit(solution)/shard_map/ppermute | solution.py:41
  71.6 7.6 %collective-permute-start.25 = (bf16[176,1024]{1,0:T(8,128)(2,1)S(1)}, bf16[176,1024]{1,0:T(8,128)(2,1)S(1)}, u32[]{:S(2)}, u32[]{:S(2)}) collective-permute-start(bf16[176,1024]{1,0:T(8,128)(2,1)S(1)} %collective-permute-done.12.refs_5_), channel_id=1, source_target_pairs={{0,1},{1,0},{2,3},{3,2},{4,5},{5,4},{6,7},{7,6},{8,9},{9,8},{10,11... | collective-permute-start | bytes 1081352 | tf_op jit(solution)/shard_map/ppermute | solution.py:41
  71.8 12.4 %collective-permute-start.21 = (bf16[176,512]{1,0:T(8,128)(2,1)S(1)}, bf16[176,512]{1,0:T(8,128)(2,1)S(1)}, u32[]{:S(2)}, u32[]{:S(2)}) collective-permute-start(bf16[176,512]{1,0:T(8,128)(2,1)S(1)} %constant_dynamic-slice_fusion), channel_id=1, source_target_pairs={{0,2},{1,15},{2,4},{3,1},{4,6},{5,3},{6,8},{7,5},{8,10},{9,7},{10,... | collective-permute-start | bytes 540680 | tf_op jit(solution)/shard_map/ppermute | solution.py:41
  75.5 8.9 %collective-permute-start.13 = (bf16[176,1024]{1,0:T(8,128)(2,1)S(1)}, bf16[176,1024]{1,0:T(8,128)(2,1)S(1)}, u32[]{:S(2)}, u32[]{:S(2)}) collective-permute-start(bf16[176,1024]{1,0:T(8,128)(2,1)S(1)} %collective-permute-done.12.refs_5_), channel_id=1, source_target_pairs={{0,2},{1,15},{2,4},{3,1},{4,6},{5,3},{6,8},{7,5},{8,10},{9,7},{10,... | collective-permute-start | bytes 1081352 | tf_op jit(solution)/shard_map/ppermute | solution.py:41
  84.3 1.5 %collective-permute-start.30 = (bf16[176,512]{1,0:T(8,128)(2,1)S(1)}, bf16[176,512]{1,0:T(8,128)(2,1)S(1)}, u32[]{:S(2)}, u32[]{:S(2)}) collective-permute-start(bf16[176,512]{1,0:T(8,128)(2,1)S(1)} %add.12), channel_id=1, source_target_pairs={{0,1},{1,0},{2,3},{3,2},{4,5},{5,4},{6,7},{7,6},{8,9},{9,8},{10,11... | collective-permute-start | bytes 540680 | tf_op jit(solution)/shard_map/ppermute | solution.py:41
  85.8 30.8 %copy-start.1 = (bf16[16,88,128]{2,1,0:T(8,128)(2,1)S(1)}, bf16[16,88,128]{2,1,0:T(8,128)(2,1)}, u32[]{:S(2)}) copy-start(bf16[16,88,128]{2,1,0:T(8,128)(2,1)} %weights.1) | copy-start | bytes 1081348
where the time goes:
time: 118 us
  starting transfers between devices  44.1 us (37%)
  waiting for transfers between devices  26.4 us (22%)
  Pallas kernels  26.2 us (22%)
  blocking collectives  20 us (17%)
    ppermute x31, starting transfers between devices, move(): return lax.ppermute(value, ('dp', 'fsdp'), pairs)  44.1 us
    ppermute x31, waiting for transfers between devices, move(): return lax.ppermute(value, ('dp', 'fsdp'), pairs)  26.4 us
    all_to_all x1, blocking collectives, body(): lax.all_to_all(current, 'dp', split_axis=0, concat_axis=0, tiled=True)  20 us
    pallas_call x1, Pallas kernels, finish(): pl.pallas_call(functools.partial(finish_kernel, [len(group) for group in...  10.8 us
    pallas_call x3, Pallas kernels, pack(): pl.pallas_call(functools.partial(pack_kernel, wide, wanted), out_shape=(j...  8.07 us
    pallas_call x1, Pallas kernels, first_gram(): pl.pallas_call(functools.partial(gram_kernel, [len(group) for group in gr...  5.02 us
  transfers between devices with their start and end apart: 31, of which 16 were waited for; matrix products, arithmetic and copies ran while one was open for 0% of the time, Pallas kernels for 9%

commit v1 on v0

--- a/solution.py
+++ b/solution.py
@@ -187,7 +187,7 @@
     core = lax.axis_index("fsdp") % 2
     copies = []
     for index, group in enumerate(groups):
-        high, wide = group[0].shape[0], target.shape[1] // HALVES
+        high, wide = target.shape[0] // RING, target.shape[1] // HALVES
         for place, piece in enumerate(group, begin):
             row, width, start = min(place, RING - 1) * high, piece.shape[1], index * wide
             if width < wide:
@@ -372,11 +372,10 @@
         parts = sums[SIDE * half : SIDE * (half + 1)]
         moment, sent = combine([parts[0]] + [second_hop(parts[k], k) for k in (1, 2, 3)])
         moments.append(moment)
-        groups.append(gather(sent, core, half == 0))
+        groups.append(gather(sent, core, True))
     stop = rows_total * 9 // 11
-    *before, zero = first_gram([groups[0][: RING - 1], groups[1][: RING - 1]], stop)
-    last = groups[1][RING - 1]
-    ends = [groups[0][RING - 1 :], [last, swap(last + zero)]]
+    *before, _ = first_gram([groups[0], groups[1][: RING - 1]], stop)
+    ends = [[], groups[1][RING - 1 :]]
     current = finish(ends, stop, moments, before)
     returned = lax.all_to_all(current, "dp", split_axis=0, concat_axis=0, tiled=True)
     return apply_update(returned, weights, 0.2 * math.sqrt(max(rows_total, cols_total)))

time: 118 us -> 114 us (0.966)
  waiting for transfers between devices: 26.4 us -> 22.2 us
    ppermute x31 -> x30, waiting for transfers between devices: 26.4 us -> 22.2 us  [move(): return lax.ppermute(value, ('dp', 'fsdp'), pairs)]
    ppermute x31 -> x30, starting transfers between devices: 44.1 us -> 43.6 us  [move(): return lax.ppermute(value, ('dp', 'fsdp'), pairs)]
  transfers between devices with their start and end apart: 31 -> 30, of which waited for: 16 -> 15; matrix products, arithmetic and copies ran while one was open for 0% -> 0% of each run, Pallas kernels for 9% -> 10%
where the time goes in v1:
time: 114 us; the launch traced here: 113 us
  starting transfers between devices  43.6 us (38%)
  Pallas kernels  26.8 us (24%)
  waiting for transfers between devices  22.2 us (19%)
  blocking collectives  19.5 us (17%)
    ppermute x30, starting transfers between devices, move(): return lax.ppermute(value, ('dp', 'fsdp'), pairs)  43.6 us
    ppermute x30, waiting for transfers between devices, move(): return lax.ppermute(value, ('dp', 'fsdp'), pairs)  22.2 us
    all_to_all x1, blocking collectives, body(): lax.all_to_all(current, 'dp', split_axis=0, concat_axis=0, tiled=True)  19.5 us
    pallas_call x1, Pallas kernels, finish(): pl.pallas_call(functools.partial(finish_kernel, [len(group) for group in...  10.8 us
    pallas_call x3, Pallas kernels, pack(): pl.pallas_call(functools.partial(pack_kernel, wide, wanted), out_shape=(j...  8.06 us
    pallas_call x1, Pallas kernels, first_gram(): pl.pallas_call(functools.partial(gram_kernel, [len(group) for group in gr...  5.6 us
  transfers between devices with their start and end apart: 30, of which 15 were waited for; matrix products, arithmetic and copies ran while one was open for 0% of the time, Pallas kernels for 10%

profile of v1, /device:TPU:64, one launch (start us, length us, event | category | flops | bytes accessed | tf_op | source)
XLA Modules:
  0.0 113.1 jit_solution(938909777670775855)
XLA Ops:
  0.6 0.0 copy-start
  0.6 2.9 %shard_map.60 = (bf16[4,88,1024]{2,1,0:T(8,128)(2,1)}, bf16[4,88,1024]{2,1,0:T(8,128)(2,1)}) custom-call(bf16[1,16,88,2048]{3,2,1,0:T(8,128)(2,1)} %grads.5, f32[16,88,128]{2,1,0:T(8,128)} %mom.5), custom_call_target="tpu_custom_call" | custom-call | bytes 2883584 | tf_op jit(solution)/shard_map/pallas_call | solution.py:98
  3.5 1.6 %collective-permute-start.1 = (bf16[4,88,1024]{2,1,0:T(8,128)(2,1)}, bf16[4,88,1024]{2,1,0:T(8,128)(2,1)S(1)}, u32[]{:S(2)}, u32[]{:S(2)}) collective-permute-start(bf16[4,88,1024]{2,1,0:T(8,128)(2,1)} %get-tuple-element.31), channel_id=1, source_target_pairs={{0,16},{1,65},{2,18},{3,67},{4,20},{5,69},{6,22},{7,71},{8,24},{9,... | collective-permute-start | bytes 2162696 | tf_op jit(solution)/shard_map/ppermute | solution.py:41
  5.1 1.7 %collective-permute-start.2 = (bf16[4,88,1024]{2,1,0:T(8,128)(2,1)}, bf16[4,88,1024]{2,1,0:T(8,128)(2,1)S(1)}, u32[]{:S(2)}, u32[]{:S(2)}) collective-permute-start(bf16[4,88,1024]{2,1,0:T(8,128)(2,1)} %get-tuple-element.33), channel_id=1, source_target_pairs={{0,48},{1,193},{2,50},{3,195},{4,52},{5,197},{6,54},{7,199},{8,56}... | collective-permute-start | bytes 2162696 | tf_op jit(solution)/shard_map/ppermute | solution.py:41
  6.9 2.8 %shard_map.59 = (bf16[4,88,1024]{2,1,0:T(8,128)(2,1)}, bf16[4,88,1024]{2,1,0:T(8,128)(2,1)}) custom-call(bf16[1,16,88,2048]{3,2,1,0:T(8,128)(2,1)} %grads.5, f32[16,88,128]{2,1,0:T(8,128)} %mom.5), custom_call_target="tpu_custom_call" | custom-call | bytes 2883584 | tf_op jit(solution)/shard_map/pallas_call | solution.py:98
  9.7 1.6 %collective-permute-start = (bf16[4,88,1024]{2,1,0:T(8,128)(2,1)}, bf16[4,88,1024]{2,1,0:T(8,128)(2,1)S(1)}, u32[]{:S(2)}, u32[]{:S(2)}) collective-permute-start(bf16[4,88,1024]{2,1,0:T(8,128)(2,1)} %get-tuple-element.29), channel_id=1, source_target_pairs={{0,48},{1,193},{2,50},{3,195},{4,52},{5,197},{6,54},{7,199},{8,56}... | collective-permute-start | bytes 2162696 | tf_op jit(solution)/shard_map/ppermute | solution.py:41
  11.3 0.5 collective-permute-start.4
  11.8 2.4 %shard_map.58 = (bf16[4,88,1024]{2,1,0:T(8,128)(2,1)S(1)}, bf16[4,88,1024]{2,1,0:T(8,128)(2,1)S(1)}, bf16[4,88,1024]{2,1,0:T(8,128)(2,1)S(1)}, bf16[4,88,1024]{2,1,0:T(8,128)(2,1)S(1)}) custom-call(bf16[1,16,88,2048]{3,2,1,0:T(8,128)(2,1)} %grads.5, f32[16,88,128]{2,1,0:T(8,128)S(1)} %copy-done), custom_call_target="tpu_custom_call" | custom-call | bytes 5767168 | tf_op jit(solution)/shard_map/pallas_call | solution.py:98
  14.1 2.2 %collective-permute-done.1.refs_1_ = bf16[4,88,1024]{2,1,0:T(8,128)(2,1)S(1)} collective-permute-done((bf16[4,88,1024]{2,1,0:T(8,128)(2,1)}, bf16[4,88,1024]{2,1,0:T(8,128)(2,1)S(1)}, u32[]{:S(2)}, u32[]{:S(2)}) %collective-permute-start.1) | collective-permute-done | bytes 720928 | tf_op jit(solution)/shard_map/ppermute | solution.py:41
  16.3 0.3 collective-permute-done.2.refs_3_
  16.6 0.3 shard_map.61
  16.9 1.6 %collective-permute-start.3 = (bf16[4,88,1024]{2,1,0:T(8,128)(2,1)S(1)}, bf16[4,88,1024]{2,1,0:T(8,128)(2,1)S(1)}, u32[]{:S(2)}, u32[]{:S(2)}) collective-permute-start(bf16[4,88,1024]{2,1,0:T(8,128)(2,1)S(1)} %get-tuple-element.34), channel_id=1, source_target_pairs={{0,16},{1,65},{2,18},{3,67},{4,20},{5,69},{6,22},{7,71},{8,24},{9,... | collective-permute-start | bytes 2162696 | tf_op jit(solution)/shard_map/ppermute | solution.py:41
  18.5 1.7 %collective-permute-start.5 = (bf16[4,88,1024]{2,1,0:T(8,128)(2,1)S(1)}, bf16[4,88,1024]{2,1,0:T(8,128)(2,1)S(1)}, u32[]{:S(2)}, u32[]{:S(2)}) collective-permute-start(bf16[4,88,1024]{2,1,0:T(8,128)(2,1)S(1)} %get-tuple-element.37), channel_id=1, source_target_pairs={{0,48},{1,193},{2,50},{3,195},{4,52},{5,197},{6,54},{7,199},{8,56}... | collective-permute-start | bytes 2162696 | tf_op jit(solution)/shard_map/ppermute | solution.py:41
  20.3 4.1 %collective-permute-done.refs_1_ = bf16[4,88,1024]{2,1,0:T(8,128)(2,1)S(1)} collective-permute-done((bf16[4,88,1024]{2,1,0:T(8,128)(2,1)}, bf16[4,88,1024]{2,1,0:T(8,128)(2,1)S(1)}, u32[]{:S(2)}, u32[]{:S(2)}) %collective-permute-start) | collective-permute-done | bytes 720928 | tf_op jit(solution)/shard_map/ppermute | solution.py:41
  24.3 0.0 collective-permute-done.4.refs_4_
  24.3 7.4 %collective-permute-done.3.refs_2_ = bf16[4,88,1024]{2,1,0:T(8,128)(2,1)S(1)} collective-permute-done((bf16[4,88,1024]{2,1,0:T(8,128)(2,1)S(1)}, bf16[4,88,1024]{2,1,0:T(8,128)(2,1)S(1)}, u32[]{:S(2)}, u32[]{:S(2)}) %collective-permute-start.3) | collective-permute-done | bytes 720928 | tf_op jit(solution)/shard_map/ppermute | solution.py:41
  31.8 0.3 collective-permute-done.5.refs_5_
  32.1 0.5 shard_map.62
  32.6 1.7 %collective-permute-start.14 = (bf16[88,1024]{1,0:T(8,128)(2,1)S(1)}, bf16[88,1024]{1,0:T(8,128)(2,1)S(1)}, u32[]{:S(2)}, u32[]{:S(2)}) collective-permute-start(bf16[88,1024]{1,0:T(8,128)(2,1)S(1)} %get-tuple-element.44), channel_id=1, source_target_pairs={{0,64},{1,17},{2,66},{3,19},{4,68},{5,21},{6,70},{7,23},{8,72},{9,... | collective-permute-start | bytes 540680 | tf_op jit(solution)/shard_map/ppermute | solution.py:41
  34.2 2.9 %collective-permute-start.15 = (bf16[88,1024]{1,0:T(8,128)(2,1)S(1)}, bf16[88,1024]{1,0:T(8,128)(2,1)S(1)}, u32[]{:S(2)}, u32[]{:S(2)}) collective-permute-start(bf16[88,1024]{1,0:T(8,128)(2,1)S(1)} %get-tuple-element.45), channel_id=1, source_target_pairs={{0,128},{1,33},{2,130},{3,35},{4,132},{5,37},{6,134},{7,39},{8,136... | collective-permute-start | bytes 540680 | tf_op jit(solution)/shard_map/ppermute | solution.py:41
  37.1 1.3 %collective-permute-start.16 = (bf16[88,1024]{1,0:T(8,128)(2,1)S(1)}, bf16[88,1024]{1,0:T(8,128)(2,1)S(1)}, u32[]{:S(2)}, u32[]{:S(2)}) collective-permute-start(bf16[88,1024]{1,0:T(8,128)(2,1)S(1)} %get-tuple-element.46), channel_id=1, source_target_pairs={{0,192},{1,49},{2,194},{3,51},{4,196},{5,53},{6,198},{7,55},{8,200... | collective-permute-start | bytes 540680 | tf_op jit(solution)/shard_map/ppermute | solution.py:41
  38.5 0.7 collective-permute-start.6
  39.2 0.8 collective-permute-start.7
  40.0 1.9 %collective-permute-start.8 = (bf16[88,1024]{1,0:T(8,128)(2,1)S(1)}, bf16[88,1024]{1,0:T(8,128)(2,1)S(1)}, u32[]{:S(2)}, u32[]{:S(2)}) collective-permute-start(bf16[88,1024]{1,0:T(8,128)(2,1)S(1)} %get-tuple-element.41), channel_id=1, source_target_pairs={{0,192},{1,49},{2,194},{3,51},{4,196},{5,53},{6,198},{7,55},{8,200... | collective-permute-start | bytes 540680 | tf_op jit(solution)/shard_map/ppermute | solution.py:41
  41.8 0.7 collective-permute-done.15.part2
  42.5 0.1 collective-permute-done.16.part3
  42.6 0.1 shard_map.64
  42.8 2.0 %collective-permute-start.18 = (bf16[88,1024]{1,0:T(8,128)(2,1)S(1)}, bf16[88,1024]{1,0:T(8,128)(2,1)S(1)}, u32[]{:S(2)}, u32[]{:S(2)}) collective-permute-start(bf16[88,1024]{1,0:T(8,128)(2,1)S(1)} %get-tuple-element.49), channel_id=1, source_target_pairs={{0,2},{1,15},{2,4},{3,1},{4,6},{5,3},{6,8},{7,5},{8,10},{9,7},{10,... | collective-permute-start | bytes 540680 | tf_op jit(solution)/shard_map/ppermute | solution.py:41
  44.8 2.4 %collective-permute-done.6.part1 = bf16[88,1024]{1,0:T(8,128)(2,1)S(1)} collective-permute-done((bf16[88,1024]{1,0:T(8,128)(2,1)S(1)}, bf16[88,1024]{1,0:T(8,128)(2,1)S(1)}, u32[]{:S(2)}, u32[]{:S(2)}) %collective-permute-start.6) | collective-permute-done | bytes 180256 | tf_op jit(solution)/shard_map/ppermute | solution.py:41
  47.1 0.0 collective-permute-done.7.part2
  47.1 0.9 collective-permute-done.8.part3
  48.0 0.1 shard_map.63
  48.2 0.3 collective-permute-start.10
  48.4 2.0 %collective-permute-start.9 = (bf16[88,1024]{1,0:T(8,128)(2,1)S(1)}, bf16[88,1024]{1,0:T(8,128)(2,1)S(1)}, u32[]{:S(2)}, u32[]{:S(2)}) collective-permute-start(bf16[88,1024]{1,0:T(8,128)(2,1)S(1)} %get-tuple-element.42), channel_id=1, source_target_pairs={{0,2},{1,15},{2,4},{3,1},{4,6},{5,3},{6,8},{7,5},{8,10},{9,7},{10,... | collective-permute-start | bytes 540680 | tf_op jit(solution)/shard_map/ppermute | solution.py:41
  50.4 0.0 collective-permute-done.18
  50.4 0.0 collective-permute-done.19
  50.5 3.2 %collective-permute-start.21 = (bf16[176,1024]{1,0:T(8,128)(2,1)S(1)}, bf16[176,1024]{1,0:T(8,128)(2,1)S(1)}, u32[]{:S(2)}, u32[]{:S(2)}) collective-permute-start(bf16[176,1024]{1,0:T(8,128)(2,1)S(1)} %pad_maximum_fusion.2.refs_1_), channel_id=1, source_target_pairs={{0,2},{1,15},{2,4},{3,1},{4,6},{5,3},{6,8},{7,5},{8,10},{9,7},{10,... | collective-permute-start | bytes 1081352 | tf_op jit(solution)/shard_map/ppermute | solution.py:41
  53.7 0.9 collective-permute-done.10
  54.7 0.6 collective-permute-done.9
  55.3 2.6 %collective-permute-start.11 = (bf16[176,1024]{1,0:T(8,128)(2,1)S(1)}, bf16[176,1024]{1,0:T(8,128)(2,1)S(1)}, u32[]{:S(2)}, u32[]{:S(2)}) collective-permute-start(bf16[176,1024]{1,0:T(8,128)(2,1)S(1)} %pad_maximum_fusion.refs_9_), channel_id=1, source_target_pairs={{0,2},{1,15},{2,4},{3,1},{4,6},{5,3},{6,8},{7,5},{8,10},{9,7},{10,... | collective-permute-start | bytes 1081352 | tf_op jit(solution)/shard_map/ppermute | solution.py:41
  58.0 0.0 collective-permute-start.26
  58.0 0.5 collective-permute-start.17
  58.5 0.0 collective-permute-start.20
  58.5 0.6 collective-permute-done.21.refs_3_
  59.1 3.1 %collective-permute-start.23 = (bf16[176,1024]{1,0:T(8,128)(2,1)S(1)}, bf16[176,1024]{1,0:T(8,128)(2,1)S(1)}, u32[]{:S(2)}, u32[]{:S(2)}) collective-permute-start(bf16[176,1024]{1,0:T(8,128)(2,1)S(1)} %collective-permute-done.21.refs_3_), channel_id=1, source_target_pairs={{0,2},{1,15},{2,4},{3,1},{4,6},{5,3},{6,8},{7,5},{8,10},{9,7},{10,... | collective-permute-start | bytes 1081352 | tf_op jit(solution)/shard_map/ppermute | solution.py:41
  62.2 0.0 collective-permute-start.27
  62.2 0.8 collective-permute-done.11.refs_11_
  63.0 3.6 %collective-permute-start.12 = (bf16[176,1024]{1,0:T(8,128)(2,1)S(1)}, bf16[176,1024]{1,0:T(8,128)(2,1)S(1)}, u32[]{:S(2)}, u32[]{:S(2)}) collective-permute-start(bf16[176,1024]{1,0:T(8,128)(2,1)S(1)} %collective-permute-done.11.refs_11_), channel_id=1, source_target_pairs={{0,2},{1,15},{2,4},{3,1},{4,6},{5,3},{6,8},{7,5},{8,10},{9,7},{10,... | collective-permute-start | bytes 1081352 | tf_op jit(solution)/shard_map/ppermute | solution.py:41
  66.6 0.0 collective-permute-done.17
  66.6 0.0 collective-permute-start.22
  66.7 0.0 collective-permute-done.20.refs_2_
  66.7 0.6 collective-permute-start.28
  67.3 3.7 %collective-permute-start.25 = (bf16[176,1024]{1,0:T(8,128)(2,1)S(1)}, bf16[176,1024]{1,0:T(8,128)(2,1)S(1)}, u32[]{:S(2)}, u32[]{:S(2)}) collective-permute-start(bf16[176,1024]{1,0:T(8,128)(2,1)S(1)} %collective-permute-done.23.refs_5_), channel_id=1, source_target_pairs={{0,2},{1,15},{2,4},{3,1},{4,6},{5,3},{6,8},{7,5},{8,10},{9,7},{10,... | collective-permute-start | bytes 1081352 | tf_op jit(solution)/shard_map/ppermute | solution.py:41
  71.0 0.6 collective-permute-done.12.refs_13_
  71.6 0.4 collective-permute-start.29
  72.0 3.6 %collective-permute-start.13 = (bf16[176,1024]{1,0:T(8,128)(2,1)S(1)}, bf16[176,1024]{1,0:T(8,128)(2,1)S(1)}, u32[]{:S(2)}, u32[]{:S(2)}) collective-permute-start(bf16[176,1024]{1,0:T(8,128)(2,1)S(1)} %collective-permute-done.12.refs_13_), channel_id=1, source_target_pairs={{0,2},{1,15},{2,4},{3,1},{4,6},{5,3},{6,8},{7,5},{8,10},{9,7},{10,... | collective-permute-start | bytes 1081352 | tf_op jit(solution)/shard_map/ppermute | solution.py:41
  75.7 0.2 collective-permute-done.25.refs_7_
  75.9 0.0 collective-permute-done.29.refs_14_
  75.9 5.6 %shard_map.65 = (bf16[1408,2048]{1,0:T(8,128)(2,1)S(1)}, bf16[1408,1408]{1,0:T(8,128)(2,1)S(1)}, bf16[176,512]{1,0:T(8,128)(2,1)}) custom-call(bf16[176,1024]{1,0:T(8,128)(2,1)S(1)} %get-tuple-element.61.refs_0_, bf16[176,1024]{1,0:T(8,128)(2,1)S(1)} %pad_maximum_fusion.2.refs_1_, bf16[176,1024]{1,0:T(8,128)(2,1)S(1)} %collective-permute-done.20.refs_2_, ...), custom_call_target="tpu_custom_call" | custom-call | flops 2717908992 | bytes 5406720 | tf_op jit(solution)/shard_map/pallas_call | solution.py:234
  81.5 0.0 collective-permute-done.13.refs_0_
  81.5 0.0 copy-start.1
  81.5 10.8 %shard_map.66 = (bf16[16,2,88,128]{3,2,1,0:T(8,128)(2,1)S(1)}, bf16[1408,2048]{1,0:T(8,128)(2,1)S(1)}, bf16[1408,1408]{1,0:T(8,128)(2,1)S(1)}) custom-call(bf16[176,1024]{1,0:T(8,128)(2,1)S(1)} %collective-permute-done.13.refs_0_, bf16[8,88,128]{2,1,0:T(8,128)(2,1)S(1)} %get-tuple-element.47.refs_1_, ...), custom_call_target="tpu_custom_call", output_to_operand_aliasing={{1}: (3, {}), {2}: (4, {})} | custom-call | flops 8595963904 | bytes 9732096 | tf_op jit(solution)/shard_map/pallas_call | solution.py:310
  92.3 19.5 %all_to_all.5.returned = bf16[16,2,88,128]{3,2,1,0:T(8,128)(2,1)S(1)} all-to-all(bf16[16,2,88,128]{3,2,1,0:T(8,128)(2,1)S(1)} %get-tuple-element.52), channel_id=1, replica_groups=mesh['dp'=16,'fsdp'=16] {'dp'}, dimensions={0} | all-to-all | bytes 1441792 | tf_op jit(solution)/shard_map/all_to_all | solution.py:380
  111.8 1.2 %shard_map.67 = (f32[16,88,128]{2,1,0:T(8,128)}, bf16[16,88,128]{2,1,0:T(8,128)(2,1)}, bf16[16,88,128]{2,1,0:T(8,128)(2,1)}) custom-call(bf16[16,2,88,128]{3,2,1,0:T(8,128)(2,1)S(1)} %all_to_all.5.returned, bf16[16,88,128]{2,1,0:T(8,128)(2,1)S(1)} %copy-done.1), custom_call_target="tpu_custom_call" | custom-call | tf_op jit(solution)/shard_map/pallas_call | solution.py:340
  (18 shorter events, 0.2 us)
Async XLA Ops:
  0.6 11.2 %copy-start = (f32[16,88,128]{2,1,0:T(8,128)S(1)}, f32[16,88,128]{2,1,0:T(8,128)}, u32[]{:S(2)}) copy-start(f32[16,88,128]{2,1,0:T(8,128)} %mom.5) | copy-start | bytes 2162692
  3.5 12.8 %collective-permute-start.1 = (bf16[4,88,1024]{2,1,0:T(8,128)(2,1)}, bf16[4,88,1024]{2,1,0:T(8,128)(2,1)S(1)}, u32[]{:S(2)}, u32[]{:S(2)}) collective-permute-start(bf16[4,88,1024]{2,1,0:T(8,128)(2,1)} %get-tuple-element.31), channel_id=1, source_target_pairs={{0,16},{1,65},{2,18},{3,67},{4,20},{5,69},{6,22},{7,71},{8,24},{9,... | collective-permute-start | bytes 2162696 | tf_op jit(solution)/shard_map/ppermute | solution.py:41
  5.1 11.5 %collective-permute-start.2 = (bf16[4,88,1024]{2,1,0:T(8,128)(2,1)}, bf16[4,88,1024]{2,1,0:T(8,128)(2,1)S(1)}, u32[]{:S(2)}, u32[]{:S(2)}) collective-permute-start(bf16[4,88,1024]{2,1,0:T(8,128)(2,1)} %get-tuple-element.33), channel_id=1, source_target_pairs={{0,48},{1,193},{2,50},{3,195},{4,52},{5,197},{6,54},{7,199},{8,56}... | collective-permute-start | bytes 2162696 | tf_op jit(solution)/shard_map/ppermute | solution.py:41
  9.7 14.7 %collective-permute-start = (bf16[4,88,1024]{2,1,0:T(8,128)(2,1)}, bf16[4,88,1024]{2,1,0:T(8,128)(2,1)S(1)}, u32[]{:S(2)}, u32[]{:S(2)}) collective-permute-start(bf16[4,88,1024]{2,1,0:T(8,128)(2,1)} %get-tuple-element.29), channel_id=1, source_target_pairs={{0,48},{1,193},{2,50},{3,195},{4,52},{5,197},{6,54},{7,199},{8,56}... | collective-permute-start | bytes 2162696 | tf_op jit(solution)/shard_map/ppermute | solution.py:41
  11.3 13.0 %collective-permute-start.4 = (bf16[4,88,1024]{2,1,0:T(8,128)(2,1)}, bf16[4,88,1024]{2,1,0:T(8,128)(2,1)S(1)}, u32[]{:S(2)}, u32[]{:S(2)}) collective-permute-start(bf16[4,88,1024]{2,1,0:T(8,128)(2,1)} %get-tuple-element.36), channel_id=1, source_target_pairs={{0,16},{1,65},{2,18},{3,67},{4,20},{5,69},{6,22},{7,71},{8,24},{9,... | collective-permute-start | bytes 2162696 | tf_op jit(solution)/shard_map/ppermute | solution.py:41
  16.9 14.8 %collective-permute-start.3 = (bf16[4,88,1024]{2,1,0:T(8,128)(2,1)S(1)}, bf16[4,88,1024]{2,1,0:T(8,128)(2,1)S(1)}, u32[]{:S(2)}, u32[]{:S(2)}) collective-permute-start(bf16[4,88,1024]{2,1,0:T(8,128)(2,1)S(1)} %get-tuple-element.34), channel_id=1, source_target_pairs={{0,16},{1,65},{2,18},{3,67},{4,20},{5,69},{6,22},{7,71},{8,24},{9,... | collective-permute-start | bytes 2162696 | tf_op jit(solution)/shard_map/ppermute | solution.py:41
  18.5 13.5 %collective-permute-start.5 = (bf16[4,88,1024]{2,1,0:T(8,128)(2,1)S(1)}, bf16[4,88,1024]{2,1,0:T(8,128)(2,1)S(1)}, u32[]{:S(2)}, u32[]{:S(2)}) collective-permute-start(bf16[4,88,1024]{2,1,0:T(8,128)(2,1)S(1)} %get-tuple-element.37), channel_id=1, source_target_pairs={{0,48},{1,193},{2,50},{3,195},{4,52},{5,197},{6,54},{7,199},{8,56}... | collective-permute-start | bytes 2162696 | tf_op jit(solution)/shard_map/ppermute | solution.py:41
  32.6 7.4 %collective-permute-start.14 = (bf16[88,1024]{1,0:T(8,128)(2,1)S(1)}, bf16[88,1024]{1,0:T(8,128)(2,1)S(1)}, u32[]{:S(2)}, u32[]{:S(2)}) collective-permute-start(bf16[88,1024]{1,0:T(8,128)(2,1)S(1)} %get-tuple-element.44), channel_id=1, source_target_pairs={{0,64},{1,17},{2,66},{3,19},{4,68},{5,21},{6,70},{7,23},{8,72},{9,... | collective-permute-start | bytes 540680 | tf_op jit(solution)/shard_map/ppermute | solution.py:41
  34.2 8.3 %collective-permute-start.15 = (bf16[88,1024]{1,0:T(8,128)(2,1)S(1)}, bf16[88,1024]{1,0:T(8,128)(2,1)S(1)}, u32[]{:S(2)}, u32[]{:S(2)}) collective-permute-start(bf16[88,1024]{1,0:T(8,128)(2,1)S(1)} %get-tuple-element.45), channel_id=1, source_target_pairs={{0,128},{1,33},{2,130},{3,35},{4,132},{5,37},{6,134},{7,39},{8,136... | collective-permute-start | bytes 540680 | tf_op jit(solution)/shard_map/ppermute | solution.py:41
  37.1 5.5 %collective-permute-start.16 = (bf16[88,1024]{1,0:T(8,128)(2,1)S(1)}, bf16[88,1024]{1,0:T(8,128)(2,1)S(1)}, u32[]{:S(2)}, u32[]{:S(2)}) collective-permute-start(bf16[88,1024]{1,0:T(8,128)(2,1)S(1)} %get-tuple-element.46), channel_id=1, source_target_pairs={{0,192},{1,49},{2,194},{3,51},{4,196},{5,53},{6,198},{7,55},{8,200... | collective-permute-start | bytes 540680 | tf_op jit(solution)/shard_map/ppermute | solution.py:41
  38.5 8.6 %collective-permute-start.6 = (bf16[88,1024]{1,0:T(8,128)(2,1)S(1)}, bf16[88,1024]{1,0:T(8,128)(2,1)S(1)}, u32[]{:S(2)}, u32[]{:S(2)}) collective-permute-start(bf16[88,1024]{1,0:T(8,128)(2,1)S(1)} %get-tuple-element.39), channel_id=1, source_target_pairs={{0,64},{1,17},{2,66},{3,19},{4,68},{5,21},{6,70},{7,23},{8,72},{9,... | collective-permute-start | bytes 540680 | tf_op jit(solution)/shard_map/ppermute | solution.py:41
  39.2 8.0 %collective-permute-start.7 = (bf16[88,1024]{1,0:T(8,128)(2,1)S(1)}, bf16[88,1024]{1,0:T(8,128)(2,1)S(1)}, u32[]{:S(2)}, u32[]{:S(2)}) collective-permute-start(bf16[88,1024]{1,0:T(8,128)(2,1)S(1)} %get-tuple-element.40), channel_id=1, source_target_pairs={{0,128},{1,33},{2,130},{3,35},{4,132},{5,37},{6,134},{7,39},{8,136... | collective-permute-start | bytes 540680 | tf_op jit(solution)/shard_map/ppermute | solution.py:41
  40.0 8.1 %collective-permute-start.8 = (bf16[88,1024]{1,0:T(8,128)(2,1)S(1)}, bf16[88,1024]{1,0:T(8,128)(2,1)S(1)}, u32[]{:S(2)}, u32[]{:S(2)}) collective-permute-start(bf16[88,1024]{1,0:T(8,128)(2,1)S(1)} %get-tuple-element.41), channel_id=1, source_target_pairs={{0,192},{1,49},{2,194},{3,51},{4,196},{5,53},{6,198},{7,55},{8,200... | collective-permute-start | bytes 540680 | tf_op jit(solution)/shard_map/ppermute | solution.py:41
  42.8 7.7 %collective-permute-start.18 = (bf16[88,1024]{1,0:T(8,128)(2,1)S(1)}, bf16[88,1024]{1,0:T(8,128)(2,1)S(1)}, u32[]{:S(2)}, u32[]{:S(2)}) collective-permute-start(bf16[88,1024]{1,0:T(8,128)(2,1)S(1)} %get-tuple-element.49), channel_id=1, source_target_pairs={{0,2},{1,15},{2,4},{3,1},{4,6},{5,3},{6,8},{7,5},{8,10},{9,7},{10,... | collective-permute-start | bytes 540680 | tf_op jit(solution)/shard_map/ppermute | solution.py:41
  44.8 5.7 %collective-permute-start.19 = (bf16[88,1024]{1,0:T(8,128)(2,1)S(1)}, bf16[88,1024]{1,0:T(8,128)(2,1)S(1)}, u32[]{:S(2)}, u32[]{:S(2)}) collective-permute-start(bf16[88,1024]{1,0:T(8,128)(2,1)S(1)} %get-tuple-element.49), channel_id=1, source_target_pairs={{0,15},{1,2},{2,1},{3,4},{4,3},{5,6},{6,5},{7,8},{8,7},{9,10},{10,... | collective-permute-start | bytes 540680 | tf_op jit(solution)/shard_map/ppermute | solution.py:41
  48.2 6.5 %collective-permute-start.10 = (bf16[88,1024]{1,0:T(8,128)(2,1)S(1)}, bf16[88,1024]{1,0:T(8,128)(2,1)S(1)}, u32[]{:S(2)}, u32[]{:S(2)}) collective-permute-start(bf16[88,1024]{1,0:T(8,128)(2,1)S(1)} %get-tuple-element.42), channel_id=1, source_target_pairs={{0,15},{1,2},{2,1},{3,4},{4,3},{5,6},{6,5},{7,8},{8,7},{9,10},{10,... | collective-permute-start | bytes 540680 | tf_op jit(solution)/shard_map/ppermute | solution.py:41
  48.4 6.8 %collective-permute-start.9 = (bf16[88,1024]{1,0:T(8,128)(2,1)S(1)}, bf16[88,1024]{1,0:T(8,128)(2,1)S(1)}, u32[]{:S(2)}, u32[]{:S(2)}) collective-permute-start(bf16[88,1024]{1,0:T(8,128)(2,1)S(1)} %get-tuple-element.42), channel_id=1, source_target_pairs={{0,2},{1,15},{2,4},{3,1},{4,6},{5,3},{6,8},{7,5},{8,10},{9,7},{10,... | collective-permute-start | bytes 540680 | tf_op jit(solution)/shard_map/ppermute | solution.py:41
  50.5 8.6 %collective-permute-start.21 = (bf16[176,1024]{1,0:T(8,128)(2,1)S(1)}, bf16[176,1024]{1,0:T(8,128)(2,1)S(1)}, u32[]{:S(2)}, u32[]{:S(2)}) collective-permute-start(bf16[176,1024]{1,0:T(8,128)(2,1)S(1)} %pad_maximum_fusion.2.refs_1_), channel_id=1, source_target_pairs={{0,2},{1,15},{2,4},{3,1},{4,6},{5,3},{6,8},{7,5},{8,10},{9,7},{10,... | collective-permute-start | bytes 1081352 | tf_op jit(solution)/shard_map/ppermute | solution.py:41
  55.3 7.7 %collective-permute-start.11 = (bf16[176,1024]{1,0:T(8,128)(2,1)S(1)}, bf16[176,1024]{1,0:T(8,128)(2,1)S(1)}, u32[]{:S(2)}, u32[]{:S(2)}) collective-permute-start(bf16[176,1024]{1,0:T(8,128)(2,1)S(1)} %pad_maximum_fusion.refs_9_), channel_id=1, source_target_pairs={{0,2},{1,15},{2,4},{3,1},{4,6},{5,3},{6,8},{7,5},{8,10},{9,7},{10,... | collective-permute-start | bytes 1081352 | tf_op jit(solution)/shard_map/ppermute | solution.py:41
  58.0 4.2 %collective-permute-start.26 = (bf16[88,1024]{1,0:T(8,128)(2,1)S(1)}, bf16[88,1024]{1,0:T(8,128)(2,1)S(1)}, u32[]{:S(2)}, u32[]{:S(2)}) collective-permute-start(bf16[88,1024]{1,0:T(8,128)(2,1)S(1)} %get-tuple-element.42), channel_id=1, source_target_pairs={{0,1},{1,0},{2,3},{3,2},{4,5},{5,4},{6,7},{7,6},{8,9},{9,8},{10,11... | collective-permute-start | bytes 540680 | tf_op jit(solution)/shard_map/ppermute | solution.py:41
  58.0 8.6 %collective-permute-start.17 = (bf16[88,1024]{1,0:T(8,128)(2,1)S(1)}, bf16[88,1024]{1,0:T(8,128)(2,1)S(1)}, u32[]{:S(2)}, u32[]{:S(2)}) collective-permute-start(bf16[88,1024]{1,0:T(8,128)(2,1)S(1)} %get-tuple-element.49), channel_id=1, source_target_pairs={{0,1},{1,0},{2,3},{3,2},{4,5},{5,4},{6,7},{7,6},{8,9},{9,8},{10,11... | collective-permute-start | bytes 540680 | tf_op jit(solution)/shard_map/ppermute | solution.py:41
  58.5 8.2 %collective-permute-start.20 = (bf16[176,1024]{1,0:T(8,128)(2,1)S(1)}, bf16[176,1024]{1,0:T(8,128)(2,1)S(1)}, u32[]{:S(2)}, u32[]{:S(2)}) collective-permute-start(bf16[176,1024]{1,0:T(8,128)(2,1)S(1)} %pad_maximum_fusion.2.refs_1_), channel_id=1, source_target_pairs={{0,1},{1,0},{2,3},{3,2},{4,5},{5,4},{6,7},{7,6},{8,9},{9,8},{10,11... | collective-permute-start | bytes 1081352 | tf_op jit(solution)/shard_map/ppermute | solution.py:41
  59.1 8.1 %collective-permute-start.23 = (bf16[176,1024]{1,0:T(8,128)(2,1)S(1)}, bf16[176,1024]{1,0:T(8,128)(2,1)S(1)}, u32[]{:S(2)}, u32[]{:S(2)}) collective-permute-start(bf16[176,1024]{1,0:T(8,128)(2,1)S(1)} %collective-permute-done.21.refs_3_), channel_id=1, source_target_pairs={{0,2},{1,15},{2,4},{3,1},{4,6},{5,3},{6,8},{7,5},{8,10},{9,7},{10,... | collective-permute-start | bytes 1081352 | tf_op jit(solution)/shard_map/ppermute | solution.py:41
  62.2 8.8 %collective-permute-start.27 = (bf16[176,1024]{1,0:T(8,128)(2,1)S(1)}, bf16[176,1024]{1,0:T(8,128)(2,1)S(1)}, u32[]{:S(2)}, u32[]{:S(2)}) collective-permute-start(bf16[176,1024]{1,0:T(8,128)(2,1)S(1)} %pad_maximum_fusion.refs_9_), channel_id=1, source_target_pairs={{0,1},{1,0},{2,3},{3,2},{4,5},{5,4},{6,7},{7,6},{8,9},{9,8},{10,11... | collective-permute-start | bytes 1081352 | tf_op jit(solution)/shard_map/ppermute | solution.py:41
  63.0 8.6 %collective-permute-start.12 = (bf16[176,1024]{1,0:T(8,128)(2,1)S(1)}, bf16[176,1024]{1,0:T(8,128)(2,1)S(1)}, u32[]{:S(2)}, u32[]{:S(2)}) collective-permute-start(bf16[176,1024]{1,0:T(8,128)(2,1)S(1)} %collective-permute-done.11.refs_11_), channel_id=1, source_target_pairs={{0,2},{1,15},{2,4},{3,1},{4,6},{5,3},{6,8},{7,5},{8,10},{9,7},{10,... | collective-permute-start | bytes 1081352 | tf_op jit(solution)/shard_map/ppermute | solution.py:41
  66.6 5.3 %collective-permute-start.22 = (bf16[176,1024]{1,0:T(8,128)(2,1)S(1)}, bf16[176,1024]{1,0:T(8,128)(2,1)S(1)}, u32[]{:S(2)}, u32[]{:S(2)}) collective-permute-start(bf16[176,1024]{1,0:T(8,128)(2,1)S(1)} %collective-permute-done.21.refs_3_), channel_id=1, source_target_pairs={{0,1},{1,0},{2,3},{3,2},{4,5},{5,4},{6,7},{7,6},{8,9},{9,8},{10,11... | collective-permute-start | bytes 1081352 | tf_op jit(solution)/shard_map/ppermute | solution.py:41
  66.7 9.0 %collective-permute-start.28 = (bf16[176,1024]{1,0:T(8,128)(2,1)S(1)}, bf16[176,1024]{1,0:T(8,128)(2,1)S(1)}, u32[]{:S(2)}, u32[]{:S(2)}) collective-permute-start(bf16[176,1024]{1,0:T(8,128)(2,1)S(1)} %collective-permute-done.11.refs_11_), channel_id=1, source_target_pairs={{0,1},{1,0},{2,3},{3,2},{4,5},{5,4},{6,7},{7,6},{8,9},{9,8},{10,11... | collective-permute-start | bytes 1081352 | tf_op jit(solution)/shard_map/ppermute | solution.py:41
  67.3 8.6 %collective-permute-start.25 = (bf16[176,1024]{1,0:T(8,128)(2,1)S(1)}, bf16[176,1024]{1,0:T(8,128)(2,1)S(1)}, u32[]{:S(2)}, u32[]{:S(2)}) collective-permute-start(bf16[176,1024]{1,0:T(8,128)(2,1)S(1)} %collective-permute-done.23.refs_5_), channel_id=1, source_target_pairs={{0,2},{1,15},{2,4},{3,1},{4,6},{5,3},{6,8},{7,5},{8,10},{9,7},{10,... | collective-permute-start | bytes 1081352 | tf_op jit(solution)/shard_map/ppermute | solution.py:41
  71.0 4.9 %collective-permute-start.24 = (bf16[176,1024]{1,0:T(8,128)(2,1)S(1)}, bf16[176,1024]{1,0:T(8,128)(2,1)S(1)}, u32[]{:S(2)}, u32[]{:S(2)}) collective-permute-start(bf16[176,1024]{1,0:T(8,128)(2,1)S(1)} %collective-permute-done.23.refs_5_), channel_id=1, source_target_pairs={{0,1},{1,0},{2,3},{3,2},{4,5},{5,4},{6,7},{7,6},{8,9},{9,8},{10,11... | collective-permute-start | bytes 1081352 | tf_op jit(solution)/shard_map/ppermute | solution.py:41
  71.6 4.3 %collective-permute-start.29 = (bf16[176,1024]{1,0:T(8,128)(2,1)S(1)}, bf16[176,1024]{1,0:T(8,128)(2,1)S(1)}, u32[]{:S(2)}, u32[]{:S(2)}) collective-permute-start(bf16[176,1024]{1,0:T(8,128)(2,1)S(1)} %collective-permute-done.12.refs_13_), channel_id=1, source_target_pairs={{0,1},{1,0},{2,3},{3,2},{4,5},{5,4},{6,7},{7,6},{8,9},{9,8},{10,11... | collective-permute-start | bytes 1081352 | tf_op jit(solution)/shard_map/ppermute | solution.py:41
  72.0 9.5 %collective-permute-start.13 = (bf16[176,1024]{1,0:T(8,128)(2,1)S(1)}, bf16[176,1024]{1,0:T(8,128)(2,1)S(1)}, u32[]{:S(2)}, u32[]{:S(2)}) collective-permute-start(bf16[176,1024]{1,0:T(8,128)(2,1)S(1)} %collective-permute-done.12.refs_13_), channel_id=1, source_target_pairs={{0,2},{1,15},{2,4},{3,1},{4,6},{5,3},{6,8},{7,5},{8,10},{9,7},{10,... | collective-permute-start | bytes 1081352 | tf_op jit(solution)/shard_map/ppermute | solution.py:41
  81.5 30.3 %copy-start.1 = (bf16[16,88,128]{2,1,0:T(8,128)(2,1)S(1)}, bf16[16,88,128]{2,1,0:T(8,128)(2,1)}, u32[]{:S(2)}) copy-start(bf16[16,88,128]{2,1,0:T(8,128)(2,1)} %weights.1) | copy-start | bytes 1081348
